TPU v7x, 256 devices: a whole 4x4x8 slice. The times are simulated.
256 devices in a mesh: mesh: 32 (over z_lo, y, core), tensor: 8 (over z_hi, x).
Axes of the slice: x: 4, y: 4, z: 8 (z_hi: 2, z_lo: 4; z = z_hi * 4 + z_lo), core: 2. Of those that a mesh axis runs over, the one named last changes fastest.
Arguments:
- cells: bfloat16 [65536, 1024], P('mesh'), may hold values from -10 to 10
- cotangent: bfloat16 [65536, 1024], P('mesh'), may hold values from -6 to 6
- counts: int32 [32], P('mesh'), may hold values from 1024 to 2048, as said below
- fx_weight: bfloat16 [1024, 1024], P(None, 'tensor'), may hold values from -0.1875 to 0.1875
- x_weight: bfloat16 [1024, 1024], P(None, 'tensor'), may hold values from -0.1875 to 0.1875
- slice_weight: bfloat16 [8, 128, 64], P('tensor'), may hold values from -0.5 to 0.5
- query_weight: float32 [8, 128, 128], P('tensor'), may hold values from -0.5 to 0.5
- key_weight: float32 [8, 128, 128], P('tensor'), may hold values from -0.5 to 0.5
- value_weight: float32 [8, 128, 128], P('tensor'), may hold values from -0.5 to 0.5
- out_weight: bfloat16 [1024, 1024], P('tensor'), may hold values from -0.1875 to 0.1875
Outputs:
- input_grad: bfloat16 [65536, 1024], P('mesh', 'tensor')
- fx_grad: float32 [1024, 1024], P(None, 'tensor')
- x_grad: float32 [1024, 1024], P(None, 'tensor')
- slice_grad: float32 [8, 128, 64], P('tensor')
- out_grad: float32 [1024, 1024], P('tensor')
Inputs may be any that keep to these rules, and one draw needn't show every extreme that they name: Block b's live cells are its first counts[b] slots; in every draw some block is full.
All inputs are finite; a program needn't handle non-finite values.
Results may differ from a plain program's by a relative error of at most 0.03.
Values may be sent and summed in bfloat16 or wider, within the bound.
A program may use at most 64 MiB of HBM per device.

v0:
```python
import jax
import jax.numpy as jnp
from jax import lax
from jax.sharding import PartitionSpec as P


def attend(tokens, query_weight, key_weight, value_weight):
    precise = lax.Precision.HIGHEST
    query = jnp.einsum("hgd,hde->hge", tokens, query_weight, precision=precise)
    keys = jnp.einsum("hgd,hde->hge", tokens, key_weight, precision=precise)
    values = jnp.einsum("hgd,hde->hge", tokens, value_weight, precision=precise)
    scores = jnp.einsum("hge,hke->hgk", query, keys, precision=precise) / jnp.sqrt(
        jnp.float32(query.shape[-1])
    )
    probs = jax.nn.softmax(scores, axis=-1)
    return jnp.einsum("hgk,hke->hge", probs, values, precision=precise)


def shards(
    cells,
    cotangent,
    counts,
    fx_weight,
    x_weight,
    slice_weight,
    query_weight,
    key_weight,
    value_weight,
    out_weight,
):
    f32 = jnp.float32
    rows = cells.shape[0]
    heads = slice_weight.shape[0]
    width = slice_weight.shape[1]
    live = (lax.iota(jnp.int32, rows) < counts[0]).astype(f32)
    feats = jnp.dot(cells, fx_weight, preferred_element_type=f32).astype(jnp.bfloat16)
    mixed = jnp.dot(cells, x_weight, preferred_element_type=f32).astype(jnp.bfloat16)
    feats3 = feats.reshape(rows, heads, width)
    mixed3 = mixed.reshape(rows, heads, width)
    logits = jnp.einsum("nhd,hdg->nhg", mixed3, slice_weight, preferred_element_type=f32)
    slice_prob = jax.nn.softmax(logits, axis=-1) * live[:, None, None]
    prob_b = slice_prob.astype(jnp.bfloat16)
    partial_sums = jnp.einsum("nhg,nhd->hgd", prob_b, feats3, preferred_element_type=f32)
    partial_totals = jnp.sum(slice_prob, axis=0)
    sums, totals = lax.psum((partial_sums, partial_totals), "mesh")
    denom = totals + 1e-05
    tokens = sums / denom[:, :, None]
    attended, attend_back = jax.vjp(attend, tokens, query_weight, key_weight, value_weight)
    attended_b = attended.astype(jnp.bfloat16)
    outputs = (
        jnp.einsum("nhg,hgd->nhd", prob_b, attended_b, preferred_element_type=f32)
        .astype(jnp.bfloat16)
        .reshape(rows, heads * width)
    )
    upstream = lax.dot_general(
        cotangent, out_weight, (((1,), (1,)), ((), ())), preferred_element_type=f32
    ).astype(jnp.bfloat16)
    contract = (((0,), (0,)), ((), ()))
    out_partial = lax.dot_general(outputs, cotangent, contract, preferred_element_type=f32)
    upstream3 = upstream.reshape(rows, heads, width)
    grad_attended = lax.psum(
        jnp.einsum("nhg,nhd->hgd", prob_b, upstream3, preferred_element_type=f32), "mesh"
    )
    grad_tokens = attend_back(grad_attended)[0]
    grad_sums = (grad_tokens / denom[:, :, None]).astype(jnp.bfloat16)
    grad_totals = -jnp.sum(grad_tokens * tokens, axis=-1) / denom
    grad_prob = (
        jnp.einsum("nhd,hgd->nhg", upstream3, attended_b, preferred_element_type=f32)
        + jnp.einsum("nhd,hgd->nhg", feats3, grad_sums, preferred_element_type=f32)
        + grad_totals[None]
    )
    grad_feats = jnp.einsum("nhg,hgd->nhd", prob_b, grad_sums, preferred_element_type=f32).astype(
        jnp.bfloat16
    )
    grad_logits = (
        slice_prob * (grad_prob - jnp.sum(slice_prob * grad_prob, axis=-1, keepdims=True))
    ).astype(jnp.bfloat16)
    grad_mixed = jnp.einsum(
        "nhg,hdg->nhd", grad_logits, slice_weight, preferred_element_type=f32
    ).astype(jnp.bfloat16)
    slice_partial = jnp.einsum("nhd,nhg->hdg", mixed3, grad_logits, preferred_element_type=f32)
    grad_feats2 = grad_feats.reshape(rows, heads * width)
    grad_mixed2 = grad_mixed.reshape(rows, heads * width)
    fx_partial = lax.dot_general(cells, grad_feats2, contract, preferred_element_type=f32)
    x_partial = lax.dot_general(cells, grad_mixed2, contract, preferred_element_type=f32)
    fx_grad, x_grad, slice_grad, out_grad = (
        lax.psum(fx_partial.astype(jnp.bfloat16), "mesh").astype(jnp.float32),
        lax.psum(x_partial.astype(jnp.bfloat16), "mesh").astype(jnp.float32),
        lax.psum(slice_partial.astype(jnp.bfloat16), "mesh").astype(jnp.float32),
        lax.psum(out_partial.astype(jnp.bfloat16), "mesh").astype(jnp.float32),
    )
    back = (((1,), (1,)), ((), ()))
    partial_input = lax.dot_general(
        grad_feats2, fx_weight, back, preferred_element_type=f32
    ) + lax.dot_general(grad_mixed2, x_weight, back, preferred_element_type=f32)
    input_grad = lax.psum_scatter(
        partial_input.astype(jnp.bfloat16), "tensor", scatter_dimension=1, tiled=True
    )
    return (input_grad, fx_grad, x_grad, slice_grad, out_grad)


def solution(mesh):
    in_specs = (
        P("mesh", None),
        P("mesh", None),
        P("mesh"),
        P(None, "tensor"),
        P(None, "tensor"),
        P("tensor", None, None),
        P("tensor", None, None),
        P("tensor", None, None),
        P("tensor", None, None),
        P("tensor", None),
    )
    out_specs = (
        P("mesh", "tensor"),
        P(None, "tensor"),
        P(None, "tensor"),
        P("tensor", None, None),
        P("tensor", None),
    )
    return jax.shard_map(shards, mesh=mesh, in_specs=in_specs, out_specs=out_specs, check_vma=False)
```

profile of v0, /device:TPU:1, one launch (start us, length us, event | category | flops | bytes accessed | tf_op | source)
XLA Modules:
  0.0 697.1 jit_solution(6418939385326696290)
XLA Ops:
  7.2 0.0 all-reduce.5.cloned.1.call-start
  8.0 3.9 convolution_convert_fusion.5
  12.0 1.3 convolution_convert_fusion.3
  13.3 0.3 fusion.43
  13.6 0.1 fusion.13
  13.7 0.7 fusion.30
  14.5 1.3 convolution_convert_fusion.4
  15.8 0.8 fusion.45
  16.6 0.8 convolution_bitcast_fusion
  17.4 0.0 all-reduce.5.cloned.1.call-update
  17.5 0.0 all-reduce.7.cloned.1.call-start
  17.5 248.6 %all-reduce.5.cloned.1.call-done = (f32[64,128]{1,0:T(8,128)}, f32[1,64,128]{2,1,0:T(8,128)}, f32[1,64]{1,0:T(1,128)}) async-done(((f32[64,128]{1,0:T(8,128)}, f32[1,64,128]{2,1,0:T(8,128)}, f32[1,64]{1,0:T(1,128)}), (f32[64,128]{1,0:T(8,128)}, f32[1,64,128]{2,1,0:T(8,128)}, f32[1,64]{1,0:T(1,128)})) %all-reduce.5.cloned.1.call-update) | async-done | bytes 65808 | tf_op jit(solution)/shard_map/psum | solution.py:61
  266.1 0.7 add_bitcast_fusion
  266.8 1.0 fusion.24
  267.8 1.0 fusion.21
  268.9 0.2 fusion.44
  269.1 1.1 fusion.37
  270.2 1.0 fusion.16
  271.2 1.0 multiply_reduce_fusion
  272.1 0.2 fusion.42
  272.3 0.9 fusion.41
  273.2 0.2 convolution_convert_fusion.9
  273.4 0.3 fusion.47
  273.7 3.8 fusion.6
  277.5 0.3 fusion.18
  277.8 0.2 convolution_add_fusion.2
  278.1 0.3 fusion.26
  278.4 0.4 fusion
  278.8 0.4 fusion.11
  279.2 0.1 fusion.14
  279.4 0.3 convolution_convert_fusion.1
  279.7 1.5 fusion.7
  281.2 1.5 fusion.8
  282.6 0.0 all-reduce.7.cloned.1.call-update
  282.7 0.0 reduce-scatter.4.cloned.1.call-start
  282.7 1.3 fusion.46
  284.0 3.3 add_convert_fusion
  287.3 6.5 copy.19
  293.8 0.0 reduce-scatter.4.cloned.1.call-update
  293.8 0.2 fusion.9
  294.0 131.7 %psum.54 = bf16[1,128,64]{1,2,0:T(8,128)(2,1)S(1)} all-reduce(bf16[1,128,64]{1,2,0:T(8,128)(2,1)S(1)} %fusion.9), channel_id=1, replica_groups=mesh['mesh'=32,'tensor'=8] {'mesh'}, use_global_device_ids=true, to_apply=%region_14.0 | all-reduce | flops 8192 | bytes 32768 | tf_op jit(solution)/shard_map/psum | solution.py:89
  425.7 0.6 convert_element_type.111
  426.3 133.7 %all-reduce.7.cloned.1.call-done = (bf16[1024,128]{0,1:T(8,128)(2,1)}, bf16[1024,128]{0,1:T(8,128)(2,1)}, bf16[128,1024]{1,0:T(8,128)(2,1)}) async-done(((bf16[1024,128]{0,1:T(8,128)(2,1)}, bf16[1024,128]{0,1:T(8,128)(2,1)}, bf16[128,1024]{1,0:T(8,128)(2,1)}), (bf16[1024,128]{0,1:T(8,128)(2,1)}, bf16[1024,128]{0,1:T(8,128)(2,1)}, bf16[128,1024]{1,0:T(8,128)(2,1)})) %all-reduce.7.cloned.1.call-update) | async-done | bytes 786448 | tf_op jit(solution)/shard_map/psum | solution.py:87
  560.1 1.9 copy.17
  562.0 1.9 copy.18
  563.8 1.8 convert_element_type.116
  565.6 122.9 %reduce-scatter.4.cloned.1.call-done = bf16[128,2048]{1,0:T(8,128)(2,1)} async-done(((bf16[1024,2048]{1,0:T(8,128)(2,1)}), bf16[128,2048]{1,0:T(8,128)(2,1)}) %reduce-scatter.4.cloned.1.call-update) | async-done | bytes 524304
  688.5 2.0 copy.20
  (31 shorter events, 0.1 us)
Async XLA Ops:
  7.2 4.8 copy-start
  7.2 258.9 %all-reduce.5.cloned.1.call-start = ((), (), s32[]{:S(2)}) async-start(), calls=%async_computation.2 | async-start | bytes 132096 | tf_op jit(solution)/shard_map/psum | solution.py:61
  7.2 4.7 copy-start.1
  12.0 1.3 copy-start.9
  12.0 2.5 copy-start.3
  12.0 2.5 copy-start.11
  13.7 253.1 %copy-start.6 = (f32[1,128,128]{2,1,0:T(8,128)S(1)}, f32[1,128,128]{2,1,0:T(8,128)}, u32[]{:S(2)}) copy-start(f32[1,128,128]{2,1,0:T(8,128)} %param.16) | copy-start | bytes 196612
  14.5 253.4 %copy-start.8 = (f32[1,128,128]{2,1,0:T(8,128)S(1)}, f32[1,128,128]{2,1,0:T(8,128)}, u32[]{:S(2)}) copy-start(f32[1,128,128]{2,1,0:T(8,128)} %param.17) | copy-start | bytes 196612
  14.5 255.7 %copy-start.7 = (f32[1,128,128]{2,1,0:T(8,128)S(1)}, f32[1,128,128]{2,1,0:T(8,128)}, u32[]{:S(2)}) copy-start(f32[1,128,128]{2,1,0:T(8,128)} %param.18) | copy-start | bytes 196612
  17.5 542.6 %all-reduce.7.cloned.1.call-start = ((), (), s32[]{:S(2)}) async-start(), calls=%async_computation.3 | async-start | bytes 1572864 | tf_op jit(solution)/shard_map/psum | solution.py:87
  266.1 11.9 %copy-start.4 = (f32[1,64,128]{2,1,0:T(8,128)S(1)}, f32[1,64,128]{2,1,0:T(8,128)}, u32[]{:S(2)}) copy-start(f32[1,64,128]{2,1,0:T(8,128)} %get-tuple-element.16) | copy-start | bytes 98308
  266.1 12.7 %copy-start.12 = (f32[1,64]{1,0:T(1,128)S(1)}, f32[1,64]{1,0:T(1,128)}, u32[]{:S(2)}) copy-start(f32[1,64]{1,0:T(1,128)} %get-tuple-element.17) | copy-start | bytes 772
  273.7 4.3 copy-start.10
  277.5 2.2 copy-start.2
  282.7 1.3 copy-start.5
  282.7 405.9 %reduce-scatter.4.cloned.1.call-start = ((), (), s32[]{:S(2)}) async-start(), calls=%async_computation.1 | async-start | bytes 4718592
Sparse Core Ops, SparseCore 0:
  17.6 248.4 all-reduce.4
  282.8 277.2 all-reduce.6
  564.3 124.2 reduce-scatter.3
where the time goes:
time: 698 us; the launch traced here: 697 us
  waiting for transfers between devices  505 us (72%)
  blocking collectives  132 us (19%)
  matrix products  28.6 us (4%)
  between operations  14.8 us (2%)
  local copies, waits for them, and re-layouts  12.4 us (2%)
    psum x1, waiting for transfers between devices, shards(): lax.psum(jnp.einsum('nhg,nhd->hgd', prob_b, upstream3, preferred_element_...  249 us
    psum x1, waiting for transfers between devices, shards(): lax.psum(fx_partial.astype(jnp.bfloat16), 'mesh').astype(jnp.float32)  134 us
    psum x1, blocking collectives, shards(): lax.psum(slice_partial.astype(jnp.bfloat16), 'mesh').astype(jnp.float32)  132 us
    unnamed x4, waiting for transfers between devices  123 us
  transfers between devices with their start and end apart: 3, of which 3 were waited for; matrix products, arithmetic and copies ran while one was open for 2% of the time, Pallas kernels for 0%

commit v1 on v0

v1 whole, which is shorter than its diff:
```python
import jax
import jax.numpy as jnp
from jax import lax
from jax.experimental import pallas as pl
from jax.experimental.pallas import tpu as pltpu
from jax.sharding import PartitionSpec as P

MESH = pl.DeviceIdType.MESH
F32 = jnp.float32
BF16 = jnp.bfloat16
ROWS = 2048
WIDTH = 1024
DIM = 128
SL = 64
CHUNK = 512
NCHUNK = ROWS // CHUNK
PEERS = [(dy, dc) for dy in range(4) for dc in range(2) if dy or dc]
NT = (((1,), (1,)), ((), ()))


def dot(a, b):
    return jnp.dot(a, b, preferred_element_type=F32)


def dot_nt(a, b):
    return lax.dot_general(a, b, NT, preferred_element_type=F32)


def precise(a, b):
    return jnp.dot(a, b, preferred_element_type=F32, precision=lax.Precision.HIGHEST)


def precise_nt(a, b):
    return lax.dot_general(
        a, b, NT, preferred_element_type=F32, precision=lax.Precision.HIGHEST
    )


class Place:
    def __init__(self):
        m = lax.axis_index("mesh")
        t = lax.axis_index("tensor")
        self.zl, self.y, self.c = lax.div(m, 8), lax.rem(lax.div(m, 2), 4), lax.rem(m, 2)
        self.zh, self.x, self.t = lax.div(t, 4), lax.rem(t, 4), t
        self.m = m
        self.g = self.y * 2 + self.c
        x, c = self.x, self.c
        self.xp = (1 - c) * (x + 1 - 2 * lax.rem(x, 2)) + c * (3 - x)
        self.xq = c * (x + 1 - 2 * lax.rem(x, 2)) + (1 - c) * (3 - x)
        self.zp = 1 - self.zh
        self.tq = self.zh * 4 + self.xq

    def peer(self, dy, dc):
        yt, ct = lax.rem(self.y + dy, 4), lax.rem(self.c + dc, 2)
        yf = lax.rem(self.y + 4 - dy, 4)
        to = (self.zl * 8 + yt * 2 + ct, self.t)
        return to, yt * 2 + ct, yf * 2 + ct

    def plane(self, d):
        zt, zf = lax.rem(self.zl + d, 4), lax.rem(self.zl + 4 - d, 4)
        return (zt * 8 + self.g, self.t), zf

    def sibling(self):
        return (self.zl * 8 + self.y * 2 + 1 - self.c, self.t)

    def across(self, x_side, z_side):
        x = self.xp if x_side else self.x
        z = self.zp if z_side else self.zh
        return (self.m, z * 4 + x)

    def other_pair(self):
        return (self.m, self.tq)


class Sends:
    def __init__(self):
        self.all = []

    def start(self, src, dst, send_sem, recv_sem, device):
        copy = pltpu.make_async_remote_copy(
            src_ref=src,
            dst_ref=dst,
            send_sem=send_sem,
            recv_sem=recv_sem,
            device_id=device,
            device_id_type=MESH,
        )
        copy.start()
        self.all.append(copy)
        return copy

    def finish(self):
        for copy in self.all:
            copy.wait_send()


class AllReduce:
    def __init__(self, place, sends, src, rbuf, zbuf, full, ss, rs):
        self.p, self.sends = place, sends
        self.src, self.rbuf, self.zbuf, self.full = src, rbuf, zbuf, full
        self.ss, self.rs = ss, rs

    def arrived(self, dst, i):
        pltpu.make_async_remote_copy(
            src_ref=dst,
            dst_ref=dst,
            send_sem=self.ss.at[i],
            recv_sem=self.rs.at[i],
            device_id=self.p.sibling(),
            device_id_type=MESH,
        ).wait_recv()

    def step1(self):
        for i, (dy, dc) in enumerate(PEERS):
            to, j, _ = self.p.peer(dy, dc)
            self.sends.start(self.src.at[j], self.rbuf.at[i], self.ss.at[i], self.rs.at[i], to)

    def step2(self):
        for i in range(7):
            self.arrived(self.rbuf.at[i], i)
        total = self.src[self.p.g].astype(F32)
        for i in range(7):
            total += self.rbuf[i].astype(F32)
        zl = self.p.zl
        self.zbuf[zl] = total.astype(self.zbuf.dtype)
        for d in range(1, 4):
            to, _ = self.p.plane(d)
            i = 6 + d
            self.sends.start(self.zbuf.at[zl], self.zbuf.at[zl], self.ss.at[i], self.rs.at[i], to)

    def step3(self):
        for d in range(1, 4):
            _, zf = self.p.plane(d)
            self.arrived(self.zbuf.at[zf], 6 + d)
        total = self.zbuf[0].astype(F32)
        for i in range(1, 4):
            total += self.zbuf[i].astype(F32)
        g = self.p.g
        self.full[g] = total.astype(self.full.dtype)
        for i, (dy, dc) in enumerate(PEERS):
            to, _, _ = self.p.peer(dy, dc)
            k = 10 + i
            self.sends.start(self.full.at[g], self.full.at[g], self.ss.at[k], self.rs.at[k], to)

    def step4(self):
        for i, (dy, dc) in enumerate(PEERS):
            _, _, j = self.p.peer(dy, dc)
            self.arrived(self.full.at[j], 10 + i)


def attention(ar_full, w3, tok_w):
    flat = ar_full[...].reshape(SL, 384)
    totals = jnp.sum(flat[:, 256:384], axis=1, keepdims=True)
    denom = totals + 1e-05
    tokens = flat[:, 0:128] / denom
    d_out = flat[:, 128:256]
    scale = 1.0 / (DIM**0.5)
    qkv = precise(tokens, w3[...])
    q, k, v = qkv[:, 0:128], qkv[:, 128:256], qkv[:, 256:384]
    s = precise_nt(q, k) * scale
    st = precise_nt(k, q) * scale
    dp = precise_nt(d_out, v)
    dpt = precise_nt(v, d_out)
    e = jnp.exp(s - jnp.max(s, axis=1, keepdims=True))
    p = e / jnp.sum(e, axis=1, keepdims=True)
    et = jnp.exp(st - jnp.max(st, axis=0, keepdims=True))
    pt = et / jnp.sum(et, axis=0, keepdims=True)
    attended = precise(p, v)
    ds = p * (dp - jnp.sum(p * dp, axis=1, keepdims=True)) * scale
    dst = pt * (dpt - jnp.sum(pt * dpt, axis=0, keepdims=True)) * scale
    dv = precise(pt, d_out)
    dq = precise(ds, k)
    dk = precise(dst, q)
    tok_w[:, 0:128] = dq
    tok_w[:, 128:256] = dk
    tok_w[:, 256:384] = dv
    grad_tokens = precise_nt(tok_w[...], w3[...])
    grad_sums = (grad_tokens / denom).astype(BF16)
    prod = grad_tokens * tokens
    col = -jnp.sum(prod, axis=1, keepdims=True) / denom
    return attended.astype(BF16), grad_sums, col


def main_kernel(
    cells_h, cot_h, counts, fx_h, xw_h, sw_h, qw_h, kw_h, vw_h, ow_h,
    out_h, px_h, pg_h, ag_h, swt_h,
    cells, cot, wa, wo, swt, sw, w3, fu, pf, st, xs, xr, outb, mt, tokw,
    acc, accb, ag, gt,
    a1r, a1z, a1f, a2s, a2r, a2z, a2f, a3s, a3r, a3z, a3f,
    lsem, csem, tsem, osem, wss, wrs, gss, grs, xss, xrs,
    s1, r1, s2, r2, s3, r3,
):
    p = Place()
    sends = Sends()
    local = []

    def load(src, dst, sem):
        copy = pltpu.make_async_copy(src, dst, sem)
        copy.start()
        return copy

    l_xw = load(xw_h, wa.at[0, :, 0:128], lsem.at[0])
    l_fx = load(fx_h, wa.at[0, :, 128:256], lsem.at[1])
    l_sw = load(sw_h.at[0], sw, lsem.at[2])
    l_ow = load(ow_h, wo.at[0], lsem.at[3])
    l_cells, l_cot = [], []
    for r in range(NCHUNK):
        rows = pl.ds(r * CHUNK, CHUNK)
        l_cells.append(load(cells_h.at[rows], cells.at[rows], csem.at[r]))
        l_cot.append(load(cot_h.at[rows], cot.at[rows], tsem.at[r]))
    l_q = load(qw_h.at[0], w3.at[:, 0:128], lsem.at[4])
    l_k = load(kw_h.at[0], w3.at[:, 128:256], lsem.at[5])
    l_v = load(vw_h.at[0], w3.at[:, 256:384], lsem.at[6])

    barrier = pltpu.get_barrier_semaphore()
    friends = [p.peer(dy, dc)[0] for dy, dc in PEERS]
    friends += [p.plane(d)[0] for d in range(1, 4)]
    friends += [p.across(0, 1), p.across(1, 0), p.across(1, 1), p.other_pair()]
    for device in friends:
        pl.semaphore_signal(barrier, inc=1, device_id=device, device_id_type=MESH)
    pl.semaphore_wait(barrier, len(friends))

    c = p.c

    def part(i, half):
        if i < 2:
            start = pl.multiple_of(half * 512 + i * 256, 256)
            return lambda slot: wa.at[slot, pl.ds(start, 256), :]
        start = pl.multiple_of(half * 64, 64)
        return lambda slot: wo.at[slot, pl.ds(start, 64), :]

    l_sw.wait()
    eye = (
        lax.broadcasted_iota(jnp.int32, (SL, SL), 0)
        == lax.broadcasted_iota(jnp.int32, (SL, SL), 1)
    )
    swt[0] = dot_nt(eye.astype(F32).astype(BF16), sw[...]).astype(BF16)
    l_xw.wait()
    l_fx.wait()
    sends.start(swt.at[0], swt.at[2], gss.at[0], grs.at[0], p.across(0, 1))
    for i in range(2):
        ref = part(i, c)
        sends.start(ref(0), ref(2), wss.at[i], wrs.at[i], p.across(0, 1))
    sends.start(swt.at[0], swt.at[1], gss.at[1], grs.at[1], p.across(1, 0))
    sends.start(wa.at[0], wa.at[1], wss.at[3], wrs.at[3], p.across(1, 0))
    l_ow.wait()
    ref = part(2, c)
    sends.start(ref(0), ref(2), wss.at[2], wrs.at[2], p.across(0, 1))
    sends.start(wo.at[0], wo.at[1], wss.at[4], wrs.at[4], p.across(1, 0))

    def arrived(dst, ssem, rsem):
        pltpu.make_async_remote_copy(
            src_ref=dst, dst_ref=dst, send_sem=ssem, recv_sem=rsem,
            device_id=p.sibling(), device_id_type=MESH,
        ).wait_recv()

    def forward_z(i):
        ref = part(i, c)
        arrived(ref(2), wss.at[i], wrs.at[i])
        sends.start(ref(2), ref(2), wss.at[5 + i], wrs.at[5 + i], p.sibling())
        sends.start(ref(2), ref(3), wss.at[8 + i], wrs.at[8 + i], p.across(1, 0))

    def forward_s(i):
        ref = part(i, 1 - c)
        arrived(ref(2), wss.at[5 + i], wrs.at[5 + i])
        sends.start(ref(2), ref(3), wss.at[11 + i], wrs.at[11 + i], p.across(1, 0))

    count = counts[0]

    def phase1(k):
        def body(r, _):
            rows = pl.ds(pl.multiple_of(r * CHUNK, CHUNK), CHUNK)
            if k == 0:
                pltpu.make_async_copy(cells_h.at[rows], cells.at[rows], csem.at[r]).wait()
            xf = dot(cells[rows, :], wa[k]).astype(BF16)
            fu[k, rows, 0:128] = xf[:, 128:256]
            logits = dot_nt(swt[k], xf[:, 0:128])
            e = jnp.exp(logits - jnp.max(logits, axis=0, keepdims=True))
            lane = lax.broadcasted_iota(jnp.int32, (1, CHUNK), 1) + r * CHUNK
            norm = jnp.where(lane < count, 1.0 / jnp.sum(e, axis=0, keepdims=True), 0.0)
            prob = e * norm
            prob_b = prob.astype(BF16)
            pf[k, :, rows] = prob
            st[k * 128 : k * 128 + 64, rows] = prob_b
            if k == 0:
                pltpu.make_async_copy(cot_h.at[rows], cot.at[rows], tsem.at[r]).wait()
            fu[k, rows, 128:256] = dot_nt(cot[rows, :], wo[k]).astype(BF16)
            if k == 0:
                acc[:, 0:256] += dot(prob_b, fu[0, rows, :])
                tot = acc[:, 256:384]
                for j in range(CHUNK // 128):
                    tot += prob[:, j * 128 : j * 128 + 128]
                acc[:, 256:384] = tot
            return 0

        lax.fori_loop(0, NCHUNK, body, 0)

    acc[...] = jnp.zeros_like(acc)
    phase1(0)
    accb[...] = acc[...].reshape(8, 8, 384)
    ar1 = AllReduce(p, sends, accb, a1r, a1z, a1f, s1, r1)
    ar1.step1()

    def products(lhs_row, rhs, dst, at):
        def body(j, _):
            cols = pl.ds(pl.multiple_of(j * 256, 256), 256)
            out = dot(st[lhs_row : lhs_row + 64, :], rhs[:, cols]).astype(BF16)
            dst[2 * j, :, at : at + 128] = out[:, 0:128]
            dst[2 * j + 1, :, at : at + 128] = out[:, 128:256]
            return 0

        lax.fori_loop(0, 4, body, 0)

    products(0, cells, a2s, 0)
    ar1.step2()
    products(0, cot, a2s, 128)
    ar2 = AllReduce(p, sends, a2s, a2r, a2z, a2f, s2, r2)
    ar1.step3()
    ar2.step1()

    arrived(swt.at[1], gss.at[1], grs.at[1])
    arrived(wa.at[1], wss.at[3], wrs.at[3])
    arrived(wo.at[1], wss.at[4], wrs.at[4])
    phase1(1)
    arrived(swt.at[2], gss.at[0], grs.at[0])
    sends.start(swt.at[2], swt.at[3], gss.at[2], grs.at[2], p.across(1, 0))
    forward_z(0)
    l_q.wait()
    l_k.wait()
    l_v.wait()
    ar1.step4()
    att, gsum, col0 = attention(a1f, w3, tokw)
    ag[0, :, 0:128] = gsum
    ag[0, :, 128:256] = att
    gt[0] = jnp.broadcast_to(jnp.sum(jnp.where(eye, col0, 0.0), axis=0, keepdims=True), (8, SL))
    for slot, device in ((1, p.across(1, 0)), (2, p.across(0, 1)), (3, p.across(1, 1))):
        i = 1 + 2 * slot
        sends.start(ag.at[0], ag.at[slot], gss.at[i], grs.at[i], device)
        sends.start(gt.at[0], gt.at[slot], gss.at[i + 1], grs.at[i + 1], device)
    forward_s(0)
    forward_z(1)
    ar2.step2()

    def phase3(k):
        row = gt[k][0:1, :]
        col = jnp.sum(jnp.where(eye, row, 0.0), axis=1, keepdims=True)

        def body(r, _):
            rows = pl.ds(pl.multiple_of(r * CHUNK, CHUNK), CHUNK)
            gp = dot_nt(ag[k], fu[k, rows, :]) + col
            prob = pf[k, :, rows]
            mean = jnp.sum(prob * gp, axis=0, keepdims=True)
            st[k * 128 + 64 : k * 128 + 128, rows] = (prob * (gp - mean)).astype(BF16)
            return 0

        lax.fori_loop(0, NCHUNK, body, 0)

    phase3(0)
    products(64, cells, a3s, 0)
    ar3 = AllReduce(p, sends, a3s, a3r, a3z, a3f, s3, r3)
    ar3.step1()
    forward_s(1)
    forward_z(2)
    ar2.step3()
    forward_s(2)
    ar3.step2()
    phase1(2)
    ar3.step3()
    arrived(swt.at[3], gss.at[2], grs.at[2])
    for i in range(3):
        arrived(part(i, c)(3), wss.at[8 + i], wrs.at[8 + i])
        arrived(part(i, 1 - c)(3), wss.at[11 + i], wrs.at[11 + i])
    phase1(3)
    for slot in (1, 2, 3):
        i = 1 + 2 * slot
        arrived(ag.at[slot], gss.at[i], grs.at[i])
        arrived(gt.at[slot], gss.at[i + 1], grs.at[i + 1])
        phase3(slot)

    def columns(slot, t):
        rows = pl.ds(pl.multiple_of(t * 128, 128), 128)
        for k in range(4):
            mt[slot, :, k * 128 : k * 128 + 64] = dot_nt(
                wa[k, rows, 128:256], ag[k, :, 0:128]
            ).astype(BF16)
            mt[slot, :, k * 128 + 64 : k * 128 + 128] = dot_nt(
                wa[k, rows, 0:128], swt[k]
            ).astype(BF16)

    columns(0, p.tq)
    for r in range(NCHUNK):
        rows = pl.ds(r * CHUNK, CHUNK)
        xs[r] = dot(mt[0], st[:, rows]).astype(BF16)
        sends.start(xs.at[r], xr.at[r], xss.at[r], xrs.at[r], p.other_pair())
    columns(1, p.t)
    outs = []
    ar2.step4()
    outs.append(load(a2f, px_h, osem.at[0]))
    outs.append(load(ag.at[0], ag_h, osem.at[1]))
    outs.append(load(swt.at[0], swt_h, osem.at[2]))
    for r in range(NCHUNK):
        rows = pl.ds(r * CHUNK, CHUNK)
        own = dot(mt[1], st[:, rows])
        arrived(xr.at[r], xss.at[r], xrs.at[r])
        total = own + xr[r].astype(F32)
        outb[rows, :] = total.T.astype(BF16)
        outs.append(load(outb.at[rows], out_h.at[rows], osem.at[4 + r]))
    ar3.step4()
    outs.append(load(a3f, pg_h, osem.at[3]))
    for copy in outs:
        copy.wait()
    sends.finish()


def finish_kernel(out_in, px, pg, ag, swt, xw, out, fx_grad, x_grad, s_grad, o_grad, sem):
    copy = pltpu.make_async_copy(out_in, out, sem)
    copy.start()
    gs, att = ag[:, 0:128], ag[:, 128:256]
    att_t = att.astype(F32).T.astype(BF16)
    swt_v = swt[...]
    total = jnp.zeros((DIM, SL), F32)
    tn = (((0,), (0,)), ((), ()))
    for j in range(8):
        cols = slice(j * 128, j * 128 + 128)
        fx_grad[cols, :] = lax.dot_general(px[j, :, 0:128], gs, tn, preferred_element_type=F32)
        o_grad[:, cols] = dot(att_t, px[j, :, 128:256])
        x_grad[cols, :] = lax.dot_general(pg[j], swt_v, tn, preferred_element_type=F32)
        total += lax.dot_general(
            xw[cols, :], pg[j], (((0,), (1,)), ((), ())), preferred_element_type=F32
        )
    s_grad[0] = total
    copy.wait()


def shards(cells, cot, counts, fx_w, x_w, s_w, q_w, k_w, v_w, o_w):
    hbm = pl.BlockSpec(memory_space=pl.ANY)
    vmem = pl.BlockSpec(memory_space=pltpu.VMEM)
    sds = jax.ShapeDtypeStruct
    dma = pltpu.SemaphoreType.DMA
    V = pltpu.VMEM
    out_t, px, pg, ag, swt = pl.pallas_call(
        main_kernel,
        name="layer",
        out_shape=(
            sds((ROWS, DIM), BF16),
            sds((8, SL, 256), BF16),
            sds((8, SL, 128), BF16),
            sds((SL, 256), BF16),
            sds((SL, 128), BF16),
        ),
        in_specs=[hbm, hbm, pl.BlockSpec(memory_space=pltpu.SMEM)] + [hbm] * 7,
        out_specs=[hbm] * 5,
        scratch_shapes=[
            V((ROWS, WIDTH), BF16),
            V((ROWS, WIDTH), BF16),
            V((4, WIDTH, 256), BF16),
            V((4, DIM, WIDTH), BF16),
            V((4, SL, 128), BF16),
            V((DIM, SL), BF16),
            V((DIM, 384), F32),
            V((4, ROWS, 256), BF16),
            V((4, SL, ROWS), F32),
            V((512, ROWS), BF16),
            V((NCHUNK, DIM, CHUNK), BF16),
            V((NCHUNK, DIM, CHUNK), BF16),
            V((ROWS, DIM), BF16),
            V((2, DIM, 512), BF16),
            V((SL, 384), F32),
            V((SL, 384), F32),
            V((8, 8, 384), F32),
            V((4, SL, 256), BF16),
            V((4, 8, SL), F32),
            V((7, 8, 384), F32),
            V((4, 8, 384), F32),
            V((8, 8, 384), F32),
            V((8, SL, 256), BF16),
            V((7, SL, 256), BF16),
            V((4, SL, 256), BF16),
            V((8, SL, 256), BF16),
            V((8, SL, 128), BF16),
            V((7, SL, 128), BF16),
            V((4, SL, 128), BF16),
            V((8, SL, 128), BF16),
            dma((7,)),
            dma((NCHUNK,)),
            dma((NCHUNK,)),
            dma((4 + NCHUNK,)),
            dma((14,)),
            dma((14,)),
            dma((9,)),
            dma((9,)),
            dma((NCHUNK,)),
            dma((NCHUNK,)),
        ]
        + [dma((17,))] * 6,
        compiler_params=pltpu.CompilerParams(
            collective_id=0, has_side_effects=True, vmem_limit_bytes=56 * 1024 * 1024
        ),
    )(cells, cot, counts, fx_w, x_w, s_w, q_w, k_w, v_w, o_w)
    return pl.pallas_call(
        finish_kernel,
        name="grads",
        out_shape=(
            sds((ROWS, DIM), BF16),
            sds((WIDTH, DIM), F32),
            sds((WIDTH, DIM), F32),
            sds((1, DIM, SL), F32),
            sds((DIM, WIDTH), F32),
        ),
        in_specs=[hbm] + [vmem] * 5,
        out_specs=[hbm] + [vmem] * 4,
        scratch_shapes=[dma],
        compiler_params=pltpu.CompilerParams(vmem_limit_bytes=32 * 1024 * 1024),
    )(out_t, px, pg, ag, swt, x_w)


def solution(mesh):
    in_specs = (
        P("mesh", None),
        P("mesh", None),
        P("mesh"),
        P(None, "tensor"),
        P(None, "tensor"),
        P("tensor", None, None),
        P("tensor", None, None),
        P("tensor", None, None),
        P("tensor", None, None),
        P("tensor", None),
    )
    out_specs = (
        P("mesh", "tensor"),
        P(None, "tensor"),
        P(None, "tensor"),
        P("tensor", None, None),
        P("tensor", None),
    )
    return jax.shard_map(shards, mesh=mesh, in_specs=in_specs, out_specs=out_specs, check_vma=False)
```

time: 698 us -> 80.3 us (0.12)
  waiting for transfers between devices: 505 us -> 0 us
  blocking collectives: 132 us -> 0 us
  Pallas kernels: 0 us -> 72.1 us
  matrix products: 28.6 us -> 0 us
  between operations: 14.8 us -> 1.32 us
    psum x2 -> x0, waiting for transfers between devices: 382 us -> none  [the longest x1 249 us: shards(): lax.psum(jnp.einsum('nhg,nhd->hgd', prob_b, upstream3, preferred_element_...]
    psum x1 -> x0, blocking collectives: 132 us -> none  [shards(): lax.psum(slice_partial.astype(jnp.bfloat16), 'mesh').astype(jnp.float32)]
    unnamed x4 -> x0, waiting for transfers between devices: 123 us -> none
    pallas_call x0 -> x2, Pallas kernels: none -> 72.1 us  [the longest x1 69.9 us: shards(): pl.pallas_call(main_kernel, name='layer', out_shape=(sds((ROWS, DIM), BF1...]
    dot_general x28 -> x0, matrix products: 28.6 us -> none  [the longest x1 3.89 us: shards(): jnp.dot(cells, x_weight, preferred_element_type=f32).astype(jnp.bfloat16)]
  transfers between devices with their start and end apart: 3 -> 0, of which waited for: 3 -> 0; matrix products, arithmetic and copies ran while one was open for 2% -> 0% of each run, Pallas kernels for 0% -> 0%
where the time goes in v1:
time: 80.3 us; the launch traced here: 79.9 us
  Pallas kernels  72.1 us (90%)
  local copies, waits for them, and re-layouts  6.5 us (8%)
  between operations  1.32 us (2%)
    pallas_call x1, Pallas kernels, shards(): pl.pallas_call(main_kernel, name='layer', out_shape=(sds((ROWS, DIM), BF1...  69.9 us
    unnamed x13, local copies, waits for them, and re-layouts  5.8 us
    pallas_call x1, Pallas kernels, shards(): pl.pallas_call(finish_kernel, name='grads', out_shape=(sds((ROWS, DIM), B...  2.24 us

profile of v1, /device:TPU:1, one launch (start us, length us, event | category | flops | bytes accessed | tf_op | source)
XLA Modules:
  0.0 79.9 jit_solution(13990433001464170511)
XLA Ops:
  1.3 1.4 %copy.15.sw_h = bf16[1,128,64]{2,1,0:T(8,128)(2,1)} copy(bf16[1,128,64]{1,2,0:T(8,128)(2,1)} %param.15) | data formatting | bytes 32768 | tf_op args[5]
  2.7 0.0 copy-start
  2.7 69.9 %layer.1 = (bf16[2048,128]{1,0:T(8,128)(2,1)}, bf16[8,64,256]{2,1,0:T(8,128)(2,1)}, bf16[8,64,128]{2,1,0:T(8,128)(2,1)}, bf16[64,256]{1,0:T(8,128)(2,1)}, bf16[64,128]{1,0:T(8,128)(2,1)}) custom-call(bf16[2048,1024]{1,0:T(8,128)(2,1)} %cells_h.1, bf16[2048,1024]{1,0:T(8,128)(2,1)} %cot_h.1, s32[1]{0:T(128)S(6)} %copy.17.counts, bf16[1024,128]{1,0:T(8,128)(2,1)} %fx_h.1, ...), custom_call_target="tpu_custom_call" | custom-call | tf_op jit(solution)/shard_map/layer/pallas_call | solution.py:441
  72.6 0.0 copy-done
  72.6 0.0 copy-start.1
  72.6 1.0 %copy-done.1 = bf16[2048,128]{1,0:T(8,128)(2,1)S(1)} copy-done((bf16[2048,128]{1,0:T(8,128)(2,1)S(1)}, bf16[2048,128]{1,0:T(8,128)(2,1)}, u32[]{:S(2)}) %copy-start.1) | copy-done | bytes 524312
  73.6 0.0 copy-start.2
  73.6 0.9 %copy-done.2 = bf16[8,64,256]{2,1,0:T(8,128)(2,1)S(1)} copy-done((bf16[8,64,256]{2,1,0:T(8,128)(2,1)S(1)}, bf16[8,64,256]{2,1,0:T(8,128)(2,1)}, u32[]{:S(2)}) %copy-start.2) | copy-done | bytes 262168
  74.6 0.0 copy-start.3
  74.6 0.9 %copy-done.3 = bf16[8,64,128]{2,1,0:T(8,128)(2,1)S(1)} copy-done((bf16[8,64,128]{2,1,0:T(8,128)(2,1)S(1)}, bf16[8,64,128]{2,1,0:T(8,128)(2,1)}, u32[]{:S(2)}) %copy-start.3) | copy-done | bytes 131096
  75.5 0.0 copy-start.4
  75.5 0.8 copy-done.4
  76.3 0.0 copy-start.5
  76.3 0.7 copy-done.5
  77.0 2.2 %grads.1 = (bf16[2048,128]{1,0:T(8,128)(2,1)}, f32[1024,128]{1,0:T(8,128)}, f32[1024,128]{1,0:T(8,128)}, f32[1,128,64]{2,1,0:T(8,128)S(1)}, f32[128,1024]{1,0:T(8,128)}) custom-call(bf16[2048,128]{1,0:T(8,128)(2,1)S(1)} %copy-done.1, bf16[8,64,256]{2,1,0:T(8,128)(2,1)S(1)} %copy-done.2, bf16[8,64,128]{2,1,0:T(8,128)(2,1)S(1)} %copy-done.3, ...), custom_call_target="tpu_custom_call" | custom-call | tf_op jit(solution)/shard_map/grads/pallas_call | solution.py:500
  79.2 0.7 copy.16
Async XLA Ops:
  2.7 69.9 %copy-start = (bf16[1024,128]{1,0:T(8,128)(2,1)S(1)}, bf16[1024,128]{1,0:T(8,128)(2,1)}, u32[]{:S(2)}) copy-start(bf16[1024,128]{1,0:T(8,128)(2,1)} %xw.1) | copy-start | bytes 786436
  72.6 1.0 %copy-start.1 = (bf16[2048,128]{1,0:T(8,128)(2,1)S(1)}, bf16[2048,128]{1,0:T(8,128)(2,1)}, u32[]{:S(2)}) copy-start(bf16[2048,128]{1,0:T(8,128)(2,1)} %get-tuple-element.10.out_in) | copy-start | bytes 1572868
  73.6 0.9 %copy-start.2 = (bf16[8,64,256]{2,1,0:T(8,128)(2,1)S(1)}, bf16[8,64,256]{2,1,0:T(8,128)(2,1)}, u32[]{:S(2)}) copy-start(bf16[8,64,256]{2,1,0:T(8,128)(2,1)} %get-tuple-element.11.px) | copy-start | bytes 786436
  74.6 0.9 %copy-start.3 = (bf16[8,64,128]{2,1,0:T(8,128)(2,1)S(1)}, bf16[8,64,128]{2,1,0:T(8,128)(2,1)}, u32[]{:S(2)}) copy-start(bf16[8,64,128]{2,1,0:T(8,128)(2,1)} %get-tuple-element.12.pg) | copy-start | bytes 393220
  75.5 0.8 copy-start.4
  76.3 0.7 copy-start.5

commit v2 on v1

v2 whole, which is shorter than its diff:
```python
import jax
import jax.numpy as jnp
from jax import lax
from jax.experimental import pallas as pl
from jax.experimental.pallas import tpu as pltpu
from jax.sharding import PartitionSpec as P

MESH = pl.DeviceIdType.MESH
F32 = jnp.float32
BF16 = jnp.bfloat16
ROWS = 2048
WIDTH = 1024
DIM = 128
SL = 64
CHUNK = 512
NCHUNK = ROWS // CHUNK
BIG = 1024
NBIG = ROWS // BIG
PEERS = [(dy, dc) for dy in range(4) for dc in range(2) if dy or dc]
NT = (((1,), (1,)), ((), ()))


def dot(a, b):
    return jnp.dot(a, b, preferred_element_type=F32)


def dot_nt(a, b):
    return lax.dot_general(a, b, NT, preferred_element_type=F32)


def precise(a, b):
    return jnp.dot(a, b, preferred_element_type=F32, precision=lax.Precision.HIGHEST)


def precise_nt(a, b):
    return lax.dot_general(
        a, b, NT, preferred_element_type=F32, precision=lax.Precision.HIGHEST
    )


class Place:
    def __init__(self):
        m = lax.axis_index("mesh")
        t = lax.axis_index("tensor")
        self.zl, self.y, self.c = lax.div(m, 8), lax.rem(lax.div(m, 2), 4), lax.rem(m, 2)
        self.zh, self.x, self.t = lax.div(t, 4), lax.rem(t, 4), t
        self.m = m
        self.g = self.y * 2 + self.c
        x, c = self.x, self.c
        self.xp = (1 - c) * (x + 1 - 2 * lax.rem(x, 2)) + c * (3 - x)
        self.xq = c * (x + 1 - 2 * lax.rem(x, 2)) + (1 - c) * (3 - x)
        self.zp = 1 - self.zh
        self.tq = self.zh * 4 + self.xq

    def peer(self, dy, dc):
        yt, ct = lax.rem(self.y + dy, 4), lax.rem(self.c + dc, 2)
        yf = lax.rem(self.y + 4 - dy, 4)
        to = (self.zl * 8 + yt * 2 + ct, self.t)
        return to, yt * 2 + ct, yf * 2 + ct

    def plane(self, d):
        zt, zf = lax.rem(self.zl + d, 4), lax.rem(self.zl + 4 - d, 4)
        return (zt * 8 + self.g, self.t), zf

    def sibling(self):
        return (self.zl * 8 + self.y * 2 + 1 - self.c, self.t)

    def across(self, x_side, z_side):
        x = self.xp if x_side else self.x
        z = self.zp if z_side else self.zh
        return (self.m, z * 4 + x)

    def other_pair(self):
        return (self.m, self.tq)


class Sends:
    def __init__(self):
        self.all = []

    def start(self, src, dst, send_sem, recv_sem, device):
        copy = pltpu.make_async_remote_copy(
            src_ref=src,
            dst_ref=dst,
            send_sem=send_sem,
            recv_sem=recv_sem,
            device_id=device,
            device_id_type=MESH,
        )
        copy.start()
        self.all.append(copy)
        return copy

    def finish(self):
        for copy in self.all:
            copy.wait_send()


class AllReduce:
    def __init__(self, place, sends, src, rbuf, zbuf, full, ss, rs):
        self.p, self.sends = place, sends
        self.src, self.rbuf, self.zbuf, self.full = src, rbuf, zbuf, full
        self.ss, self.rs = ss, rs

    def arrived(self, dst, i):
        pltpu.make_async_remote_copy(
            src_ref=dst,
            dst_ref=dst,
            send_sem=self.ss.at[i],
            recv_sem=self.rs.at[i],
            device_id=self.p.sibling(),
            device_id_type=MESH,
        ).wait_recv()

    def step1(self):
        for i, (dy, dc) in enumerate(PEERS):
            to, j, _ = self.p.peer(dy, dc)
            self.sends.start(self.src.at[j], self.rbuf.at[i], self.ss.at[i], self.rs.at[i], to)

    def step2(self):
        for i in range(7):
            self.arrived(self.rbuf.at[i], i)
        total = self.src[self.p.g].astype(F32)
        for i in range(7):
            total += self.rbuf[i].astype(F32)
        zl = self.p.zl
        self.zbuf[zl] = total.astype(self.zbuf.dtype)
        for d in range(1, 4):
            to, _ = self.p.plane(d)
            i = 6 + d
            self.sends.start(self.zbuf.at[zl], self.zbuf.at[zl], self.ss.at[i], self.rs.at[i], to)

    def step3(self):
        for d in range(1, 4):
            _, zf = self.p.plane(d)
            self.arrived(self.zbuf.at[zf], 6 + d)
        total = self.zbuf[0].astype(F32)
        for i in range(1, 4):
            total += self.zbuf[i].astype(F32)
        g = self.p.g
        self.full[g] = total.astype(self.full.dtype)
        for i, (dy, dc) in enumerate(PEERS):
            to, _, _ = self.p.peer(dy, dc)
            k = 10 + i
            self.sends.start(self.full.at[g], self.full.at[g], self.ss.at[k], self.rs.at[k], to)

    def step4(self):
        for i, (dy, dc) in enumerate(PEERS):
            _, _, j = self.p.peer(dy, dc)
            self.arrived(self.full.at[j], 10 + i)


def attention(ar_full, w3, tok_w):
    flat = ar_full[...].reshape(SL, 384)
    totals = jnp.sum(flat[:, 256:384], axis=1, keepdims=True)
    denom = totals + 1e-05
    tokens = flat[:, 0:128] / denom
    d_out = flat[:, 128:256]
    scale = 1.0 / (DIM**0.5)
    qkv = precise(tokens, w3[...])
    q, k, v = qkv[:, 0:128], qkv[:, 128:256], qkv[:, 256:384]
    s = precise_nt(q, k) * scale
    st = precise_nt(k, q) * scale
    dp = precise_nt(d_out, v)
    dpt = precise_nt(v, d_out)
    e = jnp.exp(s - jnp.max(s, axis=1, keepdims=True))
    p = e / jnp.sum(e, axis=1, keepdims=True)
    et = jnp.exp(st - jnp.max(st, axis=0, keepdims=True))
    pt = et / jnp.sum(et, axis=0, keepdims=True)
    attended = precise(p, v)
    ds = p * (dp - jnp.sum(p * dp, axis=1, keepdims=True)) * scale
    dst = pt * (dpt - jnp.sum(pt * dpt, axis=0, keepdims=True)) * scale
    dv = precise(pt, d_out)
    dq = precise(ds, k)
    dk = precise(dst, q)
    tok_w[:, 0:128] = dq
    tok_w[:, 128:256] = dk
    tok_w[:, 256:384] = dv
    grad_tokens = precise_nt(tok_w[...], w3[...])
    grad_sums = (grad_tokens / denom).astype(BF16)
    prod = grad_tokens * tokens
    col = -jnp.sum(prod, axis=1, keepdims=True) / denom
    return attended.astype(BF16), grad_sums, col


def main_kernel(
    cells_h, cot_h, counts, fx_h, xw_h, swt_h, qw_h, kw_h, vw_h, ow_h,
    out_h, px_h, pg_h, ag_h,
    cells, cot, w, wo, swt, w3, fu, pf, st, xs, xr, own, outb, mt, tokw,
    acc, accb, ag, gt, at1, at2,
    a1r, a1z, a1f, a2s, a2r, a2z, a2f, a3s, a3r, a3z, a3f,
    lsem, csem, tsem, osem, wss, wrs, gss, grs, xss, xrs,
    s1, r1, s2, r2, s3, r3,
):
    p = Place()
    sends = Sends()

    def load(src, dst, sem):
        copy = pltpu.make_async_copy(src, dst, sem)
        copy.start()
        return copy

    l_fx = load(fx_h, w.at[:, 0:128], lsem.at[0])
    l_xw = load(xw_h, w.at[:, 128:256], lsem.at[1])
    l_sw = load(swt_h.at[0], swt.at[0], lsem.at[2])
    l_ow = load(ow_h, wo.at[0], lsem.at[3])
    for r in range(NBIG):
        rows = pl.ds(r * BIG, BIG)
        load(cells_h.at[rows], cells.at[rows], csem.at[r])
        load(cot_h.at[rows], cot.at[rows], tsem.at[r])
    l_q = load(qw_h.at[0], w3.at[:, 0:128], lsem.at[4])
    l_k = load(kw_h.at[0], w3.at[:, 128:256], lsem.at[5])
    l_v = load(vw_h.at[0], w3.at[:, 256:384], lsem.at[6])

    barrier = pltpu.get_barrier_semaphore()
    friends = [p.peer(dy, dc)[0] for dy, dc in PEERS]
    friends += [p.plane(d)[0] for d in range(1, 4)]
    friends += [p.across(0, 1), p.across(1, 0), p.across(1, 1), p.other_pair()]
    for device in friends:
        pl.semaphore_signal(barrier, inc=1, device_id=device, device_id_type=MESH)
    pl.semaphore_wait(barrier, len(friends))

    c, y = p.c, p.y
    x_pair, z_pair = p.across(1, 0), p.across(0, 1)

    def start(i, src, dst, device):
        sends.start(src, dst, wss.at[i], wrs.at[i], device)

    def arrived(dst, ssem, rsem):
        pltpu.make_async_remote_copy(
            src_ref=dst, dst_ref=dst, send_sem=ssem, recv_sem=rsem,
            device_id=p.sibling(), device_id_type=MESH,
        ).wait_recv()

    def landed(i, dst):
        arrived(dst, wss.at[i], wrs.at[i])

    def w_part(core, quarter, lanes):
        rows = pl.ds(pl.multiple_of(core * 512 + quarter * 128, 128), 128)
        return w.at[rows, lanes]

    def w_half(core, lanes):
        return w.at[pl.ds(pl.multiple_of(core * 512, 512), 512), lanes]

    def wo_part(slot, core, quarter):
        return wo.at[slot, pl.ds(pl.multiple_of(core * 64 + quarter * 16, 16), 16), :]

    def wo_half(slot, core):
        return wo.at[slot, pl.ds(pl.multiple_of(core * 64, 64), 64), :]

    FX0, FX1, FX2 = slice(0, 256), slice(256, 512), slice(512, 768)
    F2, X2, X3, F3 = slice(512, 640), slice(640, 768), slice(768, 896), slice(896, 1024)

    l_fx.wait()
    l_xw.wait()
    start(0, w_part(c, y, FX0), w_part(c, y, FX2), z_pair)
    l_ow.wait()
    start(1, wo_part(0, c, y), wo_part(2, c, y), z_pair)
    l_sw.wait()
    sends.start(swt.at[0], swt.at[2], gss.at[0], grs.at[0], z_pair)
    start(2, w.at[:, FX0], w.at[:, FX1], x_pair)
    sends.start(swt.at[0], swt.at[1], gss.at[1], grs.at[1], x_pair)
    start(3, wo.at[0], wo.at[1], x_pair)

    def spread_w():
        landed(0, w_part(c, y, FX2))
        for d in range(1, 4):
            start(3 + d, w_part(c, y, FX2), w_part(c, y, FX2), p.peer(d, 0)[0])

    def spread_wo():
        landed(1, wo_part(2, c, y))
        for d in range(1, 4):
            start(6 + d, wo_part(2, c, y), wo_part(2, c, y), p.peer(d, 0)[0])

    def gather_w():
        for d in range(1, 4):
            landed(3 + d, w_part(c, lax.rem(y + 4 - d, 4), FX2))
        start(10, w_half(c, FX2), w_half(c, FX2), p.sibling())
        start(12, w_half(c, X2), w_half(c, X3), x_pair)

    def gather_wo():
        for d in range(1, 4):
            landed(6 + d, wo_part(2, c, lax.rem(y + 4 - d, 4)))
        start(11, wo_half(2, c), wo_half(2, c), p.sibling())

    def pass_on():
        landed(10, w_half(1 - c, FX2))
        start(13, w_half(1 - c, X2), w_half(1 - c, X3), x_pair)
        start(14, w_half(c, F2), w_half(c, F3), x_pair)
        start(15, wo_half(2, c), wo_half(3, c), x_pair)

    def pass_on_rest():
        landed(11, wo_half(2, 1 - c))
        start(16, w_half(1 - c, F2), w_half(1 - c, F3), x_pair)
        start(17, wo_half(2, 1 - c), wo_half(3, 1 - c), x_pair)

    count = counts[0]

    def big_rows(r):
        return pl.ds(pl.multiple_of(r * BIG, BIG), BIG)

    def softmax(k, r, mixed):
        rows = big_rows(r)
        logits = dot_nt(swt[k], mixed)
        e = jnp.exp(logits - jnp.max(logits, axis=0, keepdims=True))
        lane = lax.broadcasted_iota(jnp.int32, (1, BIG), 1) + r * BIG
        norm = jnp.where(lane < count, 1.0 / jnp.sum(e, axis=0, keepdims=True), 0.0)
        prob = e * norm
        pf[k, :, rows] = prob
        prob_b = prob.astype(BF16)
        st[k * 128 : k * 128 + 64, rows] = prob_b
        return prob, prob_b

    acc[...] = jnp.zeros_like(acc)

    def own_body(r, _):
        rows = big_rows(r)
        pltpu.make_async_copy(cells_h.at[rows], cells.at[rows], csem.at[r]).wait()
        xf = dot(cells[rows, :], w[:, FX0]).astype(BF16)
        fu[rows, 0:128] = xf[:, 0:128]
        prob, prob_b = softmax(0, r, xf[:, 128:256])
        pltpu.make_async_copy(cot_h.at[rows], cot.at[rows], tsem.at[r]).wait()
        fu[rows, 128:256] = dot_nt(cot[rows, :], wo[0]).astype(BF16)
        acc[:, 0:256] += dot(prob_b, fu[rows, :])
        tot = acc[:, 256:384]
        for j in range(BIG // 128):
            tot += prob[:, j * 128 : j * 128 + 128]
        acc[:, 256:384] = tot
        return 0

    lax.fori_loop(0, NBIG, own_body, 0)
    accb[...] = acc[...].reshape(8, 8, 384)
    ar1 = AllReduce(p, sends, accb, a1r, a1z, a1f, s1, r1)
    ar2 = AllReduce(p, sends, a2s, a2r, a2z, a2f, s2, r2)
    ar3 = AllReduce(p, sends, a3s, a3r, a3z, a3f, s3, r3)
    ar1.step1()

    def products(lhs_row, rhs, dst, at):
        def body(j, _):
            cols = pl.ds(pl.multiple_of(j * 512, 512), 512)
            out = dot(st[lhs_row : lhs_row + 64, :], rhs[:, cols]).astype(BF16)
            for i in range(4):
                dst[4 * j + i, :, at : at + 128] = out[:, i * 128 : i * 128 + 128]
            return 0

        lax.fori_loop(0, 2, body, 0)

    products(0, cells, a2s, 0)
    spread_w()
    products(0, cot, a2s, 128)
    spread_wo()
    ar1.step2()
    arrived(swt.at[2], gss.at[0], grs.at[0])
    sends.start(swt.at[2], swt.at[3], gss.at[2], grs.at[2], x_pair)
    arrived(swt.at[1], gss.at[1], grs.at[1])
    landed(2, w.at[:, FX1])

    def pair_body(r, _):
        mixed = dot(cells[big_rows(r), :], w[:, 384:512]).astype(BF16)
        softmax(1, r, mixed)
        return 0

    lax.fori_loop(0, NBIG, pair_body, 0)
    ar1.step3()
    gather_w()
    ar2.step1()
    gather_wo()
    landed(3, wo.at[1])
    pass_on()
    l_q.wait()
    l_k.wait()
    l_v.wait()
    ar1.step4()
    att, gsum, col0 = attention(a1f, w3, tokw)
    ag[0, :, 0:128] = gsum
    ag[0, :, 128:256] = att
    eye = (
        lax.broadcasted_iota(jnp.int32, (SL, SL), 0)
        == lax.broadcasted_iota(jnp.int32, (SL, SL), 1)
    )
    gt[0] = jnp.broadcast_to(jnp.sum(jnp.where(eye, col0, 0.0), axis=0, keepdims=True), (8, SL))
    for slot, device in ((3, p.across(1, 1)), (2, z_pair), (1, x_pair)):
        i = 1 + 2 * slot
        sends.start(ag.at[0], ag.at[slot], gss.at[i], grs.at[i], device)
        sends.start(gt.at[0], gt.at[slot], gss.at[i + 1], grs.at[i + 1], device)
    pass_on_rest()

    def vjp(k, rows, gp):
        prob = pf[k, :, rows]
        mean = jnp.sum(prob * gp, axis=0, keepdims=True)
        st[k * 128 + 64 : k * 128 + 128, rows] = (prob * (gp - mean)).astype(BF16)

    def own_vjp(r, _):
        rows = big_rows(r)
        vjp(0, rows, dot_nt(ag[0], fu[rows, :]) + col0)
        return 0

    lax.fori_loop(0, NBIG, own_vjp, 0)
    products(64, cells, a3s, 0)
    ar3.step1()
    ar2.step2()
    arrived(swt.at[3], gss.at[2], grs.at[2])
    landed(12, w_half(c, X3))
    landed(13, w_half(1 - c, X3))

    def far_body(r, _):
        mixed = dot(cells[big_rows(r), :], w[:, 640:896]).astype(BF16)
        softmax(2, r, mixed[:, 0:128])
        softmax(3, r, mixed[:, 128:256])
        return 0

    lax.fori_loop(0, NBIG, far_body, 0)
    ar2.step3()
    ar3.step2()

    f_at = (0, 256, 512, 896)
    x_at = (128, 384, 640, 768)
    col_rows = [pl.ds(pl.multiple_of(t * 128, 128), 128) for t in (p.tq, p.t)]

    def fixed_columns(k):
        for i, rows in enumerate(col_rows):
            mt[i, :, k * 128 + 64 : k * 128 + 128] = dot_nt(
                w[rows, x_at[k] : x_at[k] + 128], swt[k]
            ).astype(BF16)

    def sum_columns(k):
        for i, rows in enumerate(col_rows):
            mt[i, :, k * 128 : k * 128 + 64] = dot_nt(
                w[rows, f_at[k] : f_at[k] + 128], ag[k, :, 0:128]
            ).astype(BF16)

    def fold(k):
        i = 1 + 2 * k
        arrived(ag.at[k], gss.at[i], grs.at[i])
        arrived(gt.at[k], gss.at[i + 1], grs.at[i + 1])
        full = ag[k].astype(F32)
        centred = (full - jnp.mean(full, axis=0, keepdims=True)).astype(BF16)
        rows = slice((k - 1) * 64, k * 64)
        at1[rows, :] = dot_nt(centred[:, 0:128], w[:, f_at[k] : f_at[k] + 128]).astype(BF16)
        at2[rows, :] = dot(centred[:, 128:256], wo[k]).astype(BF16)
        sum_columns(k)

    for k in range(4):
        fixed_columns(k)
    sum_columns(0)
    fold(1)
    landed(14, w_half(c, F3))
    landed(15, wo_half(3, c))
    landed(16, w_half(1 - c, F3))
    landed(17, wo_half(3, 1 - c))
    fold(2)
    fold(3)
    gcol = [
        jnp.sum(jnp.where(eye, gt[k][0:1, :], 0.0), axis=1, keepdims=True) for k in (1, 2, 3)
    ]
    for r in range(NCHUNK):
        rows = pl.ds(r * CHUNK, CHUNK)
        gp = dot_nt(at1[...], cells[rows, :]) + dot_nt(at2[...], cot[rows, :])
        for k in (1, 2, 3):
            vjp(k, rows, gp[(k - 1) * 64 : k * 64, :] + gcol[k - 1])
        xs[r] = dot(mt[0], st[:, rows]).astype(BF16)
        sends.start(xs.at[r], xr.at[r], xss.at[r], xrs.at[r], p.other_pair())
    ar3.step3()
    outs = [load(ag.at[0], ag_h, osem.at[0])]
    ar2.step4()
    outs.append(load(a2f, px_h, osem.at[1]))
    for r in range(NCHUNK):
        rows = pl.ds(r * CHUNK, CHUNK)
        own[:, rows] = dot(mt[1], st[:, rows])
    for r in range(NCHUNK):
        rows = pl.ds(r * CHUNK, CHUNK)
        arrived(xr.at[r], xss.at[r], xrs.at[r])
        total = own[:, rows] + xr[r].astype(F32)
        outb[rows, :] = total.T.astype(BF16)
        outs.append(load(outb.at[rows], out_h.at[rows], osem.at[3 + r]))
    ar3.step4()
    outs.append(load(a3f, pg_h, osem.at[2]))
    for copy in outs:
        copy.wait()
    sends.finish()


def finish_kernel(
    out_in, px_h, pg_h, ag_h, swt_h, xw_h,
    out, fx_h, xg_h, sg_h, og_h,
    held, px, pg, ag, swt, xw, fx, xg, sg, og, sem,
):
    copies = []

    def move(src, dst, i):
        copy = pltpu.make_async_copy(src, dst, sem.at[i])
        copy.start()
        return copy

    l_px, l_ag = move(px_h, px, 0), move(ag_h, ag, 1)
    l_pg, l_swt, l_xw = move(pg_h, pg, 2), move(swt_h, swt, 3), move(xw_h, xw, 4)
    l_out = move(out_in, held, 5)
    l_px.wait()
    l_ag.wait()
    gs, att = ag[:, 0:128], ag[:, 128:256]
    att_t = att.astype(F32).T.astype(BF16)
    tn = (((0,), (0,)), ((), ()))
    for j in range(8):
        cols = slice(j * 128, j * 128 + 128)
        fx[cols, :] = lax.dot_general(px[j, :, 0:128], gs, tn, preferred_element_type=F32)
    copies.append(move(fx, fx_h, 6))
    l_out.wait()
    copies.append(move(held, out, 10))
    for j in range(8):
        cols = slice(j * 128, j * 128 + 128)
        og[:, cols] = dot(att_t, px[j, :, 128:256])
    copies.append(move(og, og_h, 7))
    l_pg.wait()
    l_swt.wait()
    swt_v = swt[0]
    for j in range(8):
        cols = slice(j * 128, j * 128 + 128)
        xg[cols, :] = lax.dot_general(pg[j], swt_v, tn, preferred_element_type=F32)
    copies.append(move(xg, xg_h, 8))
    l_xw.wait()
    total = jnp.zeros((SL, DIM), F32)
    for j in range(8):
        total += dot(pg[j], xw[j * 128 : j * 128 + 128, :])
    sg[0] = total
    copies.append(move(sg, sg_h, 9))
    for copy in copies:
        copy.wait()


def shards(cells, cot, counts, fx_w, x_w, s_w, q_w, k_w, v_w, o_w):
    hbm = pl.BlockSpec(memory_space=pl.ANY)
    sds = jax.ShapeDtypeStruct
    dma = pltpu.SemaphoreType.DMA
    V = pltpu.VMEM
    swt = jnp.swapaxes(s_w, 1, 2)
    limit = 60 * 1024 * 1024
    out, px, pg, ag = pl.pallas_call(
        main_kernel,
        name="layer",
        out_shape=(
            sds((ROWS, DIM), BF16),
            sds((8, SL, 256), BF16),
            sds((8, SL, 128), BF16),
            sds((SL, 256), BF16),
        ),
        in_specs=[hbm, hbm, pl.BlockSpec(memory_space=pltpu.SMEM)] + [hbm] * 7,
        out_specs=[hbm] * 4,
        scratch_shapes=[
            V((ROWS, WIDTH), BF16),
            V((ROWS, WIDTH), BF16),
            V((WIDTH, 1024), BF16),
            V((4, DIM, WIDTH), BF16),
            V((4, SL, 128), BF16),
            V((DIM, 384), F32),
            V((ROWS, 256), BF16),
            V((4, SL, ROWS), F32),
            V((512, ROWS), BF16),
            V((NCHUNK, DIM, CHUNK), BF16),
            V((NCHUNK, DIM, CHUNK), BF16),
            V((DIM, ROWS), F32),
            V((ROWS, DIM), BF16),
            V((2, DIM, 512), BF16),
            V((SL, 384), F32),
            V((SL, 384), F32),
            V((8, 8, 384), F32),
            V((4, SL, 256), BF16),
            V((4, 8, SL), F32),
            V((192, WIDTH), BF16),
            V((192, WIDTH), BF16),
            V((7, 8, 384), F32),
            V((4, 8, 384), F32),
            V((8, 8, 384), F32),
            V((8, SL, 256), BF16),
            V((7, SL, 256), BF16),
            V((4, SL, 256), BF16),
            V((8, SL, 256), BF16),
            V((8, SL, 128), BF16),
            V((7, SL, 128), BF16),
            V((4, SL, 128), BF16),
            V((8, SL, 128), BF16),
            dma((7,)),
            dma((NBIG,)),
            dma((NBIG,)),
            dma((3 + NCHUNK,)),
            dma((18,)),
            dma((18,)),
            dma((9,)),
            dma((9,)),
            dma((NCHUNK,)),
            dma((NCHUNK,)),
        ]
        + [dma((17,))] * 6,
        compiler_params=pltpu.CompilerParams(
            collective_id=0, has_side_effects=True, vmem_limit_bytes=limit
        ),
    )(cells, cot, counts, fx_w, x_w, swt, q_w, k_w, v_w, o_w)
    outs = pl.pallas_call(
        finish_kernel,
        name="grads",
        out_shape=(
            sds((ROWS, DIM), BF16),
            sds((WIDTH, DIM), F32),
            sds((WIDTH, DIM), F32),
            sds((1, SL, DIM), F32),
            sds((DIM, WIDTH), F32),
        ),
        in_specs=[hbm] * 6,
        out_specs=[hbm] * 5,
        scratch_shapes=[
            V((ROWS, DIM), BF16),
            V((8, SL, 256), BF16),
            V((8, SL, 128), BF16),
            V((SL, 256), BF16),
            V((1, SL, 128), BF16),
            V((WIDTH, DIM), BF16),
            V((WIDTH, DIM), F32),
            V((WIDTH, DIM), F32),
            V((1, SL, DIM), F32),
            V((DIM, WIDTH), F32),
            dma((11,)),
        ],
        compiler_params=pltpu.CompilerParams(vmem_limit_bytes=limit),
    )(out, px, pg, ag, swt, x_w)
    return outs[0], outs[1], outs[2], jnp.swapaxes(outs[3], 1, 2), outs[4]


def solution(mesh):
    in_specs = (
        P("mesh", None),
        P("mesh", None),
        P("mesh"),
        P(None, "tensor"),
        P(None, "tensor"),
        P("tensor", None, None),
        P("tensor", None, None),
        P("tensor", None, None),
        P("tensor", None, None),
        P("tensor", None),
    )
    out_specs = (
        P("mesh", "tensor"),
        P(None, "tensor"),
        P(None, "tensor"),
        P("tensor", None, None),
        P("tensor", None),
    )
    return jax.shard_map(shards, mesh=mesh, in_specs=in_specs, out_specs=out_specs, check_vma=False)
```

time: 80.3 us -> 54.7 us (0.68)
  Pallas kernels: 72.1 us -> 53.3 us
  local copies, waits for them, and re-layouts: 6.5 us -> 0 us
    pallas_call x1, Pallas kernels: 69.9 us -> 50.6 us  [shards(): pl.pallas_call(main_kernel, name='layer', out_shape=(sds((ROWS, DIM), BF1...]
    unnamed x13 -> x0, local copies, waits for them, and re-layouts: 5.8 us -> none
where the time goes in v2:
time: 54.7 us; the launch traced here: 54.6 us
  Pallas kernels  53.3 us (97%)
  between operations  1.29 us (2%)
    pallas_call x1, Pallas kernels, shards(): pl.pallas_call(main_kernel, name='layer', out_shape=(sds((ROWS, DIM), BF1...  50.6 us
    pallas_call x1, Pallas kernels, shards(): pl.pallas_call(finish_kernel, name='grads', out_shape=(sds((ROWS, DIM), B...  2.74 us

profile of v2, /device:TPU:1, one launch (start us, length us, event | category | flops | bytes accessed | tf_op | source)
XLA Modules:
  0.0 54.6 jit_solution(14774292991112624651)
XLA Ops:
  1.3 50.6 %layer.1 = (bf16[2048,128]{1,0:T(8,128)(2,1)}, bf16[8,64,256]{2,1,0:T(8,128)(2,1)}, bf16[8,64,128]{2,1,0:T(8,128)(2,1)}, bf16[64,256]{1,0:T(8,128)(2,1)}) custom-call(bf16[2048,1024]{1,0:T(8,128)(2,1)} %cells_h.1, bf16[2048,1024]{1,0:T(8,128)(2,1)} %cot_h.1, s32[1]{0:T(128)S(6)} %copy.15.counts, bf16[1024,128]{1,0:T(8,128)(2,1)} %fx_h.1, ...), custom_call_target="tpu_custom_call" | custom-call | tf_op jit(solution)/shard_map/layer/pallas_call | solution.py:537
  51.9 2.7 %grads.1 = (bf16[2048,128]{1,0:T(8,128)(2,1)}, f32[1024,128]{1,0:T(8,128)}, f32[1024,128]{1,0:T(8,128)}, f32[1,64,128]{2,1,0:T(8,128)}, f32[128,1024]{1,0:T(8,128)}) custom-call(bf16[2048,128]{1,0:T(8,128)(2,1)} %get-tuple-element.14.out_in, bf16[8,64,256]{2,1,0:T(8,128)(2,1)} %get-tuple-element.15.px_h, bf16[8,64,128]{2,1,0:T(8,128)(2,1)} %get-tuple-element.16.pg_h, ...), custom_call_target="tpu_custom_call" | custom-call | tf_op jit(solution)/shard_map/grads/pallas_call | solution.py:597

commit v3 on v2

--- a/solution.py
+++ b/solution.py
@@ -14,6 +14,8 @@
 SL = 64
 CHUNK = 512
 NCHUNK = ROWS // CHUNK
+EDGES = (0, 512, 1024, 1536, 2048)
+NLATE = len(EDGES) - 1
 BIG = 1024
 NBIG = ROWS // BIG
 PEERS = [(dy, dc) for dy in range(4) for dc in range(2) if dy or dc]
@@ -94,6 +96,7 @@
     def finish(self):
         for copy in self.all:
             copy.wait_send()
+        self.all = []
 
 
 class AllReduce:
@@ -150,7 +153,7 @@
             self.arrived(self.full.at[j], 10 + i)
 
 
-def attention(ar_full, w3, tok_w):
+def attention(ar_full, w3, tok_w, on_attended):
     flat = ar_full[...].reshape(SL, 384)
     totals = jnp.sum(flat[:, 256:384], axis=1, keepdims=True)
     denom = totals + 1e-05
@@ -167,7 +170,7 @@
     p = e / jnp.sum(e, axis=1, keepdims=True)
     et = jnp.exp(st - jnp.max(st, axis=0, keepdims=True))
     pt = et / jnp.sum(et, axis=0, keepdims=True)
-    attended = precise(p, v)
+    on_attended(precise(p, v).astype(BF16))
     ds = p * (dp - jnp.sum(p * dp, axis=1, keepdims=True)) * scale
     dst = pt * (dpt - jnp.sum(pt * dpt, axis=0, keepdims=True)) * scale
     dv = precise(pt, d_out)
@@ -180,13 +183,13 @@
     grad_sums = (grad_tokens / denom).astype(BF16)
     prod = grad_tokens * tokens
     col = -jnp.sum(prod, axis=1, keepdims=True) / denom
-    return attended.astype(BF16), grad_sums, col
+    return grad_sums, col
 
 
 def main_kernel(
     cells_h, cot_h, counts, fx_h, xw_h, swt_h, qw_h, kw_h, vw_h, ow_h,
-    out_h, px_h, pg_h, ag_h,
-    cells, cot, w, wo, swt, w3, fu, pf, st, xs, xr, own, outb, mt, tokw,
+    out_h, fxg_h, xg_h, sg_h, og_h,
+    cells, cot, w, wo, swt, w3, fu, pf, st, xs, xr, own, outb, fxg, xg, sg, og, mt, tokw,
     acc, accb, ag, gt, at1, at2,
     a1r, a1z, a1f, a2s, a2r, a2z, a2f, a3s, a3r, a3z, a3f,
     lsem, csem, tsem, osem, wss, wrs, gss, grs, xss, xrs,
@@ -194,6 +197,7 @@
 ):
     p = Place()
     sends = Sends()
+    last = Sends()
 
     def load(src, dst, sem):
         copy = pltpu.make_async_copy(src, dst, sem)
@@ -204,10 +208,11 @@
     l_xw = load(xw_h, w.at[:, 128:256], lsem.at[1])
     l_sw = load(swt_h.at[0], swt.at[0], lsem.at[2])
     l_ow = load(ow_h, wo.at[0], lsem.at[3])
-    for r in range(NBIG):
-        rows = pl.ds(r * BIG, BIG)
-        load(cells_h.at[rows], cells.at[rows], csem.at[r])
-        load(cot_h.at[rows], cot.at[rows], tsem.at[r])
+    l_cells, l_cot = [], []
+    for r in range(NCHUNK):
+        rows = pl.ds(r * CHUNK, CHUNK)
+        l_cells.append(load(cells_h.at[rows], cells.at[rows], csem.at[r]))
+        l_cot.append(load(cot_h.at[rows], cot.at[rows], tsem.at[r]))
     l_q = load(qw_h.at[0], w3.at[:, 0:128], lsem.at[4])
     l_k = load(kw_h.at[0], w3.at[:, 128:256], lsem.at[5])
     l_v = load(vw_h.at[0], w3.at[:, 256:384], lsem.at[6])
@@ -218,7 +223,6 @@
     friends += [p.across(0, 1), p.across(1, 0), p.across(1, 1), p.other_pair()]
     for device in friends:
         pl.semaphore_signal(barrier, inc=1, device_id=device, device_id_type=MESH)
-    pl.semaphore_wait(barrier, len(friends))
 
     c, y = p.c, p.y
     x_pair, z_pair = p.across(1, 0), p.across(0, 1)
@@ -251,17 +255,6 @@
     FX0, FX1, FX2 = slice(0, 256), slice(256, 512), slice(512, 768)
     F2, X2, X3, F3 = slice(512, 640), slice(640, 768), slice(768, 896), slice(896, 1024)
 
-    l_fx.wait()
-    l_xw.wait()
-    start(0, w_part(c, y, FX0), w_part(c, y, FX2), z_pair)
-    l_ow.wait()
-    start(1, wo_part(0, c, y), wo_part(2, c, y), z_pair)
-    l_sw.wait()
-    sends.start(swt.at[0], swt.at[2], gss.at[0], grs.at[0], z_pair)
-    start(2, w.at[:, FX0], w.at[:, FX1], x_pair)
-    sends.start(swt.at[0], swt.at[1], gss.at[1], grs.at[1], x_pair)
-    start(3, wo.at[0], wo.at[1], x_pair)
-
     def spread_w():
         landed(0, w_part(c, y, FX2))
         for d in range(1, 4):
@@ -299,11 +292,11 @@
     def big_rows(r):
         return pl.ds(pl.multiple_of(r * BIG, BIG), BIG)
 
-    def softmax(k, r, mixed):
-        rows = big_rows(r)
+    def softmax(k, first, size, mixed):
+        rows = pl.ds(first, size)
         logits = dot_nt(swt[k], mixed)
         e = jnp.exp(logits - jnp.max(logits, axis=0, keepdims=True))
-        lane = lax.broadcasted_iota(jnp.int32, (1, BIG), 1) + r * BIG
+        lane = lax.broadcasted_iota(jnp.int32, (1, size), 1) + first
         norm = jnp.where(lane < count, 1.0 / jnp.sum(e, axis=0, keepdims=True), 0.0)
         prob = e * norm
         pf[k, :, rows] = prob
@@ -313,22 +306,36 @@
 
     acc[...] = jnp.zeros_like(acc)
 
-    def own_body(r, _):
-        rows = big_rows(r)
-        pltpu.make_async_copy(cells_h.at[rows], cells.at[rows], csem.at[r]).wait()
+    def own_rows(first, size):
+        rows = pl.ds(first, size)
+        parts = range(first // CHUNK, (first + size) // CHUNK)
+        for r in parts:
+            l_cells[r].wait()
         xf = dot(cells[rows, :], w[:, FX0]).astype(BF16)
-        fu[rows, 0:128] = xf[:, 0:128]
-        prob, prob_b = softmax(0, r, xf[:, 128:256])
-        pltpu.make_async_copy(cot_h.at[rows], cot.at[rows], tsem.at[r]).wait()
-        fu[rows, 128:256] = dot_nt(cot[rows, :], wo[0]).astype(BF16)
-        acc[:, 0:256] += dot(prob_b, fu[rows, :])
+        fu[0, rows, 0:128] = xf[:, 0:128]
+        prob, prob_b = softmax(0, first, size, xf[:, 128:256])
+        for r in parts:
+            l_cot[r].wait()
+        fu[0, rows, 128:256] = dot_nt(cot[rows, :], wo[0]).astype(BF16)
+        acc[:, 0:256] += dot(prob_b, fu[0, rows, :])
         tot = acc[:, 256:384]
-        for j in range(BIG // 128):
+        for j in range(size // 128):
             tot += prob[:, j * 128 : j * 128 + 128]
         acc[:, 256:384] = tot
-        return 0
-
-    lax.fori_loop(0, NBIG, own_body, 0)
+
+    l_fx.wait()
+    l_xw.wait()
+    l_sw.wait()
+    l_ow.wait()
+    own_rows(0, CHUNK)
+    pl.semaphore_wait(barrier, len(friends))
+    start(0, w_part(c, y, FX0), w_part(c, y, FX2), z_pair)
+    start(1, wo_part(0, c, y), wo_part(2, c, y), z_pair)
+    sends.start(swt.at[0], swt.at[2], gss.at[0], grs.at[0], z_pair)
+    start(2, w.at[:, FX0], w.at[:, FX1], x_pair)
+    sends.start(swt.at[0], swt.at[1], gss.at[1], grs.at[1], x_pair)
+    start(3, wo.at[0], wo.at[1], x_pair)
+    own_rows(CHUNK, ROWS - CHUNK)
     accb[...] = acc[...].reshape(8, 8, 384)
     ar1 = AllReduce(p, sends, accb, a1r, a1z, a1f, s1, r1)
     ar2 = AllReduce(p, sends, a2s, a2r, a2z, a2f, s2, r2)
@@ -347,42 +354,53 @@
 
     products(0, cells, a2s, 0)
     spread_w()
+    ar1.step2()
+    spread_wo()
     products(0, cot, a2s, 128)
-    spread_wo()
-    ar1.step2()
     arrived(swt.at[2], gss.at[0], grs.at[0])
     sends.start(swt.at[2], swt.at[3], gss.at[2], grs.at[2], x_pair)
+    def pair_body(r, _):
+        rows = big_rows(r)
+        xf = dot(cells[rows, :], w[:, FX1]).astype(BF16)
+        fu[1, rows, 0:128] = xf[:, 0:128]
+        softmax(1, pl.multiple_of(r * BIG, BIG), BIG, xf[:, 128:256])
+        fu[1, rows, 128:256] = dot_nt(cot[rows, :], wo[1]).astype(BF16)
+        return 0
+
+    ar1.step3()
     arrived(swt.at[1], gss.at[1], grs.at[1])
     landed(2, w.at[:, FX1])
-
-    def pair_body(r, _):
-        mixed = dot(cells[big_rows(r), :], w[:, 384:512]).astype(BF16)
-        softmax(1, r, mixed)
-        return 0
-
-    lax.fori_loop(0, NBIG, pair_body, 0)
-    ar1.step3()
+    landed(3, wo.at[1])
+    pair_body(0, 0)
     gather_w()
-    ar2.step1()
     gather_wo()
-    landed(3, wo.at[1])
+    pair_body(1, 0)
     pass_on()
     l_q.wait()
     l_k.wait()
     l_v.wait()
     ar1.step4()
-    att, gsum, col0 = attention(a1f, w3, tokw)
-    ag[0, :, 0:128] = gsum
-    ag[0, :, 128:256] = att
+    readers = ((3, p.across(1, 1)), (2, z_pair), (1, x_pair))
+    GS, ATT = slice(0, 128), slice(128, 256)
+
+    def on_attended(att):
+        ag[0, :, ATT] = att
+        for slot, device in readers:
+            i = 8 + slot
+            sends.start(ag.at[0, :, ATT], ag.at[slot, :, ATT], gss.at[i], grs.at[i], device)
+
+    gsum, col0 = attention(a1f, w3, tokw, on_attended)
+    ag[0, :, GS] = gsum
     eye = (
         lax.broadcasted_iota(jnp.int32, (SL, SL), 0)
         == lax.broadcasted_iota(jnp.int32, (SL, SL), 1)
     )
     gt[0] = jnp.broadcast_to(jnp.sum(jnp.where(eye, col0, 0.0), axis=0, keepdims=True), (8, SL))
-    for slot, device in ((3, p.across(1, 1)), (2, z_pair), (1, x_pair)):
+    for slot, device in readers:
         i = 1 + 2 * slot
-        sends.start(ag.at[0], ag.at[slot], gss.at[i], grs.at[i], device)
+        sends.start(ag.at[0, :, GS], ag.at[slot, :, GS], gss.at[i], grs.at[i], device)
         sends.start(gt.at[0], gt.at[slot], gss.at[i + 1], grs.at[i + 1], device)
+    ar2.step1()
     pass_on_rest()
 
     def vjp(k, rows, gp):
@@ -390,28 +408,33 @@
         mean = jnp.sum(prob * gp, axis=0, keepdims=True)
         st[k * 128 + 64 : k * 128 + 128, rows] = (prob * (gp - mean)).astype(BF16)
 
-    def own_vjp(r, _):
-        rows = big_rows(r)
-        vjp(0, rows, dot_nt(ag[0], fu[rows, :]) + col0)
-        return 0
-
-    lax.fori_loop(0, NBIG, own_vjp, 0)
+    def near_vjp(k, col):
+        def body(r, _):
+            rows = big_rows(r)
+            vjp(k, rows, dot_nt(ag[k], fu[k, rows, :]) + col)
+            return 0
+
+        lax.fori_loop(0, NBIG, body, 0)
+
+    def column(k):
+        return jnp.sum(jnp.where(eye, gt[k][0:1, :], 0.0), axis=1, keepdims=True)
+
+    near_vjp(0, col0)
     products(64, cells, a3s, 0)
     ar3.step1()
-    ar2.step2()
     arrived(swt.at[3], gss.at[2], grs.at[2])
     landed(12, w_half(c, X3))
     landed(13, w_half(1 - c, X3))
 
     def far_body(r, _):
         mixed = dot(cells[big_rows(r), :], w[:, 640:896]).astype(BF16)
-        softmax(2, r, mixed[:, 0:128])
-        softmax(3, r, mixed[:, 128:256])
+        first = pl.multiple_of(r * BIG, BIG)
+        softmax(2, first, BIG, mixed[:, 0:128])
+        softmax(3, first, BIG, mixed[:, 128:256])
         return 0
 
     lax.fori_loop(0, NBIG, far_body, 0)
-    ar2.step3()
-    ar3.step2()
+    ar2.step2()
 
     f_at = (0, 256, 512, 896)
     x_at = (128, 384, 640, 768)
@@ -429,101 +452,103 @@
                 w[rows, f_at[k] : f_at[k] + 128], ag[k, :, 0:128]
             ).astype(BF16)
 
-    def fold(k):
+    def attended_from(k):
+        arrived(ag.at[k, :, ATT], gss.at[8 + k], grs.at[8 + k])
+
+    def gradients_from(k):
         i = 1 + 2 * k
-        arrived(ag.at[k], gss.at[i], grs.at[i])
+        arrived(ag.at[k, :, GS], gss.at[i], grs.at[i])
         arrived(gt.at[k], gss.at[i + 1], grs.at[i + 1])
-        full = ag[k].astype(F32)
-        centred = (full - jnp.mean(full, axis=0, keepdims=True)).astype(BF16)
-        rows = slice((k - 1) * 64, k * 64)
-        at1[rows, :] = dot_nt(centred[:, 0:128], w[:, f_at[k] : f_at[k] + 128]).astype(BF16)
-        at2[rows, :] = dot(centred[:, 128:256], wo[k]).astype(BF16)
-        sum_columns(k)
+
+    def centred(k, lanes):
+        full = ag[k, :, lanes].astype(F32)
+        return (full - jnp.mean(full, axis=0, keepdims=True)).astype(BF16)
+
+    def fold_rows(k):
+        return slice((k - 2) * 64, (k - 1) * 64)
 
     for k in range(4):
         fixed_columns(k)
     sum_columns(0)
-    fold(1)
+    ar3.step2()
+    attended_from(1)
+    gradients_from(1)
+    near_vjp(1, column(1))
+    sum_columns(1)
     landed(14, w_half(c, F3))
     landed(15, wo_half(3, c))
     landed(16, w_half(1 - c, F3))
     landed(17, wo_half(3, 1 - c))
-    fold(2)
-    fold(3)
-    gcol = [
-        jnp.sum(jnp.where(eye, gt[k][0:1, :], 0.0), axis=1, keepdims=True) for k in (1, 2, 3)
-    ]
-    for r in range(NCHUNK):
-        rows = pl.ds(r * CHUNK, CHUNK)
+    attended_from(2)
+    attended_from(3)
+    for k in (2, 3):
+        at2[fold_rows(k), :] = dot(centred(k, ATT), wo[k]).astype(BF16)
+    gradients_from(2)
+    gradients_from(3)
+    for k in (2, 3):
+        lanes = slice(f_at[k], f_at[k] + 128)
+        at1[fold_rows(k), :] = dot_nt(centred(k, GS), w[:, lanes]).astype(BF16)
+    for k in (2, 3):
+        sum_columns(k)
+    gcol = [column(k) for k in (2, 3)]
+    for r in range(NLATE):
+        rows = pl.ds(EDGES[r], EDGES[r + 1] - EDGES[r])
         gp = dot_nt(at1[...], cells[rows, :]) + dot_nt(at2[...], cot[rows, :])
-        for k in (1, 2, 3):
-            vjp(k, rows, gp[(k - 1) * 64 : k * 64, :] + gcol[k - 1])
-        xs[r] = dot(mt[0], st[:, rows]).astype(BF16)
-        sends.start(xs.at[r], xr.at[r], xss.at[r], xrs.at[r], p.other_pair())
+        for k in (2, 3):
+            vjp(k, rows, gp[(k - 2) * 64 : (k - 1) * 64, :] + gcol[k - 2])
+        xs[:, rows] = dot(mt[0], st[:, rows]).astype(BF16)
+        part = slice(EDGES[r], EDGES[r + 1])
+        last.start(xs.at[:, part], xr.at[:, part], xss.at[r], xrs.at[r], p.other_pair())
+        if r == 1:
+            ar2.step3()
     ar3.step3()
-    outs = [load(ag.at[0], ag_h, osem.at[0])]
-    ar2.step4()
-    outs.append(load(a2f, px_h, osem.at[1]))
     for r in range(NCHUNK):
         rows = pl.ds(r * CHUNK, CHUNK)
         own[:, rows] = dot(mt[1], st[:, rows])
-    for r in range(NCHUNK):
-        rows = pl.ds(r * CHUNK, CHUNK)
-        arrived(xr.at[r], xss.at[r], xrs.at[r])
-        total = own[:, rows] + xr[r].astype(F32)
+    tn = (((0,), (0,)), ((), ()))
+    outs = []
+    ar2.step4()
+    gs = ag[0, :, 0:128]
+    att_t = ag[0, :, 128:256].astype(F32).T.astype(BF16)
+    for j in range(8):
+        cols = slice(j * 128, j * 128 + 128)
+        fxg[cols, :] = lax.dot_general(a2f[j, :, 0:128], gs, tn, preferred_element_type=F32)
+        og[:, cols] = dot(att_t, a2f[j, :, 128:256])
+    outs.append(load(fxg, fxg_h, osem.at[0]))
+    outs.append(load(og, og_h, osem.at[1]))
+    for r in range(NLATE):
+        rows = pl.ds(EDGES[r], EDGES[r + 1] - EDGES[r])
+        arrived(xr.at[:, slice(EDGES[r], EDGES[r + 1])], xss.at[r], xrs.at[r])
+        total = own[:, rows] + xr[:, rows].astype(F32)
         outb[rows, :] = total.T.astype(BF16)
-        outs.append(load(outb.at[rows], out_h.at[rows], osem.at[3 + r]))
-    ar3.step4()
-    outs.append(load(a3f, pg_h, osem.at[2]))
+        outs.append(load(outb.at[rows], out_h.at[rows], osem.at[4 + r]))
+        if r == 2:
+            ar3.step4()
+            swt0 = swt[0]
+            total = jnp.zeros((SL, DIM), F32)
+            for j in range(8):
+                cols = slice(j * 128, j * 128 + 128)
+                xg[cols, :] = lax.dot_general(a3f[j], swt0, tn, preferred_element_type=F32)
+                total += dot(a3f[j], w[cols, 128:256])
+            sg[0] = total
+            outs.append(load(xg, xg_h, osem.at[2]))
+            outs.append(load(sg, sg_h, osem.at[3]))
+            sends.finish()
     for copy in outs:
         copy.wait()
-    sends.finish()
-
-
-def finish_kernel(
-    out_in, px_h, pg_h, ag_h, swt_h, xw_h,
-    out, fx_h, xg_h, sg_h, og_h,
-    held, px, pg, ag, swt, xw, fx, xg, sg, og, sem,
-):
-    copies = []
-
-    def move(src, dst, i):
-        copy = pltpu.make_async_copy(src, dst, sem.at[i])
+    last.finish()
+
+
+def finish_kernel(*refs):
+    src, dst, held, sem = refs[0:5], refs[5:10], refs[10:15], refs[15]
+    inward = [pltpu.make_async_copy(src[i], held[i], sem.at[i]) for i in range(5)]
+    outward = [pltpu.make_async_copy(held[i], dst[i], sem.at[5 + i]) for i in range(5)]
+    for copy in inward:
         copy.start()
-        return copy
-
-    l_px, l_ag = move(px_h, px, 0), move(ag_h, ag, 1)
-    l_pg, l_swt, l_xw = move(pg_h, pg, 2), move(swt_h, swt, 3), move(xw_h, xw, 4)
-    l_out = move(out_in, held, 5)
-    l_px.wait()
-    l_ag.wait()
-    gs, att = ag[:, 0:128], ag[:, 128:256]
-    att_t = att.astype(F32).T.astype(BF16)
-    tn = (((0,), (0,)), ((), ()))
-    for j in range(8):
-        cols = slice(j * 128, j * 128 + 128)
-        fx[cols, :] = lax.dot_general(px[j, :, 0:128], gs, tn, preferred_element_type=F32)
-    copies.append(move(fx, fx_h, 6))
-    l_out.wait()
-    copies.append(move(held, out, 10))
-    for j in range(8):
-        cols = slice(j * 128, j * 128 + 128)
-        og[:, cols] = dot(att_t, px[j, :, 128:256])
-    copies.append(move(og, og_h, 7))
-    l_pg.wait()
-    l_swt.wait()
-    swt_v = swt[0]
-    for j in range(8):
-        cols = slice(j * 128, j * 128 + 128)
-        xg[cols, :] = lax.dot_general(pg[j], swt_v, tn, preferred_element_type=F32)
-    copies.append(move(xg, xg_h, 8))
-    l_xw.wait()
-    total = jnp.zeros((SL, DIM), F32)
-    for j in range(8):
-        total += dot(pg[j], xw[j * 128 : j * 128 + 128, :])
-    sg[0] = total
-    copies.append(move(sg, sg_h, 9))
-    for copy in copies:
+    for i in range(5):
+        inward[i].wait()
+        outward[i].start()
+    for copy in outward:
         copy.wait()
 
 
@@ -534,17 +559,20 @@
     V = pltpu.VMEM
     swt = jnp.swapaxes(s_w, 1, 2)
     limit = 60 * 1024 * 1024
-    out, px, pg, ag = pl.pallas_call(
+    shapes = (
+        sds((ROWS, DIM), BF16),
+        sds((WIDTH, DIM), F32),
+        sds((WIDTH, DIM), F32),
+        sds((1, SL, DIM), F32),
+        sds((DIM, WIDTH), F32),
+    )
+    held = [V(a.shape, a.dtype) for a in shapes]
+    outs = pl.pallas_call(
         main_kernel,
         name="layer",
-        out_shape=(
-            sds((ROWS, DIM), BF16),
-            sds((8, SL, 256), BF16),
-            sds((8, SL, 128), BF16),
-            sds((SL, 256), BF16),
-        ),
+        out_shape=shapes,
         in_specs=[hbm, hbm, pl.BlockSpec(memory_space=pltpu.SMEM)] + [hbm] * 7,
-        out_specs=[hbm] * 4,
+        out_specs=[hbm] * 5,
         scratch_shapes=[
             V((ROWS, WIDTH), BF16),
             V((ROWS, WIDTH), BF16),
@@ -552,21 +580,21 @@
             V((4, DIM, WIDTH), BF16),
             V((4, SL, 128), BF16),
             V((DIM, 384), F32),
-            V((ROWS, 256), BF16),
+            V((2, ROWS, 256), BF16),
             V((4, SL, ROWS), F32),
             V((512, ROWS), BF16),
-            V((NCHUNK, DIM, CHUNK), BF16),
-            V((NCHUNK, DIM, CHUNK), BF16),
+            V((DIM, ROWS), BF16),
+            V((DIM, ROWS), BF16),
             V((DIM, ROWS), F32),
-            V((ROWS, DIM), BF16),
+            *held,
             V((2, DIM, 512), BF16),
             V((SL, 384), F32),
             V((SL, 384), F32),
             V((8, 8, 384), F32),
             V((4, SL, 256), BF16),
             V((4, 8, SL), F32),
-            V((192, WIDTH), BF16),
-            V((192, WIDTH), BF16),
+            V((128, WIDTH), BF16),
+            V((128, WIDTH), BF16),
             V((7, 8, 384), F32),
             V((4, 8, 384), F32),
             V((8, 8, 384), F32),
@@ -579,15 +607,15 @@
             V((4, SL, 128), BF16),
             V((8, SL, 128), BF16),
             dma((7,)),
-            dma((NBIG,)),
-            dma((NBIG,)),
-            dma((3 + NCHUNK,)),
+            dma((NCHUNK,)),
+            dma((NCHUNK,)),
+            dma((4 + NLATE,)),
             dma((18,)),
             dma((18,)),
-            dma((9,)),
-            dma((9,)),
-            dma((NCHUNK,)),
-            dma((NCHUNK,)),
+            dma((12,)),
+            dma((12,)),
+            dma((NLATE,)),
+            dma((NLATE,)),
         ]
         + [dma((17,))] * 6,
         compiler_params=pltpu.CompilerParams(
@@ -597,30 +625,12 @@
     outs = pl.pallas_call(
         finish_kernel,
         name="grads",
-        out_shape=(
-            sds((ROWS, DIM), BF16),
-            sds((WIDTH, DIM), F32),
-            sds((WIDTH, DIM), F32),
-            sds((1, SL, DIM), F32),
-            sds((DIM, WIDTH), F32),
-        ),
-        in_specs=[hbm] * 6,
+        out_shape=shapes,
+        in_specs=[hbm] * 5,
         out_specs=[hbm] * 5,
-        scratch_shapes=[
-            V((ROWS, DIM), BF16),
-            V((8, SL, 256), BF16),
-            V((8, SL, 128), BF16),
-            V((SL, 256), BF16),
-            V((1, SL, 128), BF16),
-            V((WIDTH, DIM), BF16),
-            V((WIDTH, DIM), F32),
-            V((WIDTH, DIM), F32),
-            V((1, SL, DIM), F32),
-            V((DIM, WIDTH), F32),
-            dma((11,)),
-        ],
+        scratch_shapes=[*held, dma((10,))],
         compiler_params=pltpu.CompilerParams(vmem_limit_bytes=limit),
-    )(out, px, pg, ag, swt, x_w)
+    )(*outs)
     return outs[0], outs[1], outs[2], jnp.swapaxes(outs[3], 1, 2), outs[4]
 
 

time: 54.7 us -> 54 us (0.987)
  Pallas kernels: 53.3 us -> 52.4 us
    pallas_call x2, Pallas kernels: 53.3 us -> 52.4 us  [the longest x1 50 us: shards(): pl.pallas_call(main_kernel, name='layer', out_shape=shapes, in_specs=[hbm...]
where the time goes in v3:
time: 54 us; the launch traced here: 53.9 us
  Pallas kernels  52.4 us (97%)
  between operations  1.45 us (3%)
    pallas_call x1, Pallas kernels, shards(): pl.pallas_call(main_kernel, name='layer', out_shape=shapes, in_specs=[hbm...  50 us
    pallas_call x1, Pallas kernels, shards(): pl.pallas_call(finish_kernel, name='grads', out_shape=shapes, in_specs=[h...  2.45 us

profile of v3, /device:TPU:1, one launch (start us, length us, event | category | flops | bytes accessed | tf_op | source)
XLA Modules:
  0.0 53.9 jit_solution(12062356385777379656)
XLA Ops:
  1.3 50.0 %layer.1 = (bf16[2048,128]{1,0:T(8,128)(2,1)}, f32[1024,128]{1,0:T(8,128)}, f32[1024,128]{1,0:T(8,128)}, f32[1,64,128]{2,1,0:T(8,128)}, f32[128,1024]{1,0:T(8,128)}) custom-call(bf16[2048,1024]{1,0:T(8,128)(2,1)} %cells_h.1, bf16[2048,1024]{1,0:T(8,128)(2,1)} %cot_h.1, s32[1]{0:T(128)S(6)} %copy.15.counts, bf16[1024,128]{1,0:T(8,128)(2,1)} %fx_h.1, ...), custom_call_target="tpu_custom_call" | custom-call | tf_op jit(solution)/shard_map/layer/pallas_call | solution.py:570
  51.2 2.5 %grads.1 = (bf16[2048,128]{1,0:T(8,128)(2,1)}, f32[1024,128]{1,0:T(8,128)}, f32[1024,128]{1,0:T(8,128)}, f32[1,64,128]{2,1,0:T(8,128)}, f32[128,1024]{1,0:T(8,128)}) custom-call(bf16[2048,128]{1,0:T(8,128)(2,1)} %get-tuple-element.15.refs_0_, f32[1024,128]{1,0:T(8,128)} %get-tuple-element.16.refs_1_, f32[1024,128]{1,0:T(8,128)} %get-tuple-element.17.refs_2_, ...), custom_call_target="tpu_custom_call" | custom-call | tf_op jit(solution)/shard_map/grads/pallas_call | solution.py:625

commit v4 on v3

--- a/solution.py
+++ b/solution.py
@@ -18,7 +18,7 @@
 NLATE = len(EDGES) - 1
 BIG = 1024
 NBIG = ROWS // BIG
-PEERS = [(dy, dc) for dy in range(4) for dc in range(2) if dy or dc]
+PEERS = [(2, 1), (2, 0), (1, 1), (3, 1), (1, 0), (3, 0), (0, 1)]
 NT = (((1,), (1,)), ((), ()))
 
 
@@ -259,17 +259,23 @@
         landed(0, w_part(c, y, FX2))
         for d in range(1, 4):
             start(3 + d, w_part(c, y, FX2), w_part(c, y, FX2), p.peer(d, 0)[0])
+        start(12, w_part(c, y, X2), w_part(c, y, X3), x_pair)
+        start(14, w_part(c, y, F2), w_part(c, y, F3), x_pair)
 
     def spread_wo():
         landed(1, wo_part(2, c, y))
         for d in range(1, 4):
             start(6 + d, wo_part(2, c, y), wo_part(2, c, y), p.peer(d, 0)[0])
+        start(15, wo_part(2, c, y), wo_part(3, c, y), x_pair)
+
+    quarters = [(d, lax.rem(y + 4 - d, 4)) for d in range(1, 4)]
 
     def gather_w():
         for d in range(1, 4):
             landed(3 + d, w_part(c, lax.rem(y + 4 - d, 4), FX2))
         start(10, w_half(c, FX2), w_half(c, FX2), p.sibling())
-        start(12, w_half(c, X2), w_half(c, X3), x_pair)
+        for d, q in quarters:
+            start(17 + d, w_part(c, q, X2), w_part(c, q, X3), x_pair)
 
     def gather_wo():
         for d in range(1, 4):
@@ -279,8 +285,9 @@
     def pass_on():
         landed(10, w_half(1 - c, FX2))
         start(13, w_half(1 - c, X2), w_half(1 - c, X3), x_pair)
-        start(14, w_half(c, F2), w_half(c, F3), x_pair)
-        start(15, wo_half(2, c), wo_half(3, c), x_pair)
+        for d, q in quarters:
+            start(20 + d, w_part(c, q, F2), w_part(c, q, F3), x_pair)
+            start(23 + d, wo_part(2, c, q), wo_part(3, c, q), x_pair)
 
     def pass_on_rest():
         landed(11, wo_half(2, 1 - c))
@@ -423,7 +430,9 @@
     products(64, cells, a3s, 0)
     ar3.step1()
     arrived(swt.at[3], gss.at[2], grs.at[2])
-    landed(12, w_half(c, X3))
+    landed(12, w_part(c, y, X3))
+    for d, q in quarters:
+        landed(17 + d, w_part(c, q, X3))
     landed(13, w_half(1 - c, X3))
 
     def far_body(r, _):
@@ -475,8 +484,11 @@
     gradients_from(1)
     near_vjp(1, column(1))
     sum_columns(1)
-    landed(14, w_half(c, F3))
-    landed(15, wo_half(3, c))
+    landed(14, w_part(c, y, F3))
+    landed(15, wo_part(3, c, y))
+    for d, q in quarters:
+        landed(20 + d, w_part(c, q, F3))
+        landed(23 + d, wo_part(3, c, q))
     landed(16, w_half(1 - c, F3))
     landed(17, wo_half(3, 1 - c))
     attended_from(2)
@@ -610,8 +622,8 @@
             dma((NCHUNK,)),
             dma((NCHUNK,)),
             dma((4 + NLATE,)),
-            dma((18,)),
-            dma((18,)),
+            dma((27,)),
+            dma((27,)),
             dma((12,)),
             dma((12,)),
             dma((NLATE,)),

time: 54 us -> 53.7 us (level)
  no operation moved by 1% of the time
where the time goes in v4:
time: 53.7 us; the launch traced here: 53.6 us
  Pallas kernels  52.1 us (97%)
  between operations  1.45 us (3%)
    pallas_call x1, Pallas kernels, shards(): pl.pallas_call(main_kernel, name='layer', out_shape=shapes, in_specs=[hbm...  49.7 us
    pallas_call x1, Pallas kernels, shards(): pl.pallas_call(finish_kernel, name='grads', out_shape=shapes, in_specs=[h...  2.45 us

profile of v4, /device:TPU:1, one launch (start us, length us, event | category | flops | bytes accessed | tf_op | source)
XLA Modules:
  0.0 53.6 jit_solution(18128473294075076280)
XLA Ops:
  1.3 49.7 %layer.1 = (bf16[2048,128]{1,0:T(8,128)(2,1)}, f32[1024,128]{1,0:T(8,128)}, f32[1024,128]{1,0:T(8,128)}, f32[1,64,128]{2,1,0:T(8,128)}, f32[128,1024]{1,0:T(8,128)}) custom-call(bf16[2048,1024]{1,0:T(8,128)(2,1)} %cells_h.1, bf16[2048,1024]{1,0:T(8,128)(2,1)} %cot_h.1, s32[1]{0:T(128)S(6)} %copy.15.counts, bf16[1024,128]{1,0:T(8,128)(2,1)} %fx_h.1, ...), custom_call_target="tpu_custom_call" | custom-call | tf_op jit(solution)/shard_map/layer/pallas_call | solution.py:582
  51.0 2.5 %grads.1 = (bf16[2048,128]{1,0:T(8,128)(2,1)}, f32[1024,128]{1,0:T(8,128)}, f32[1024,128]{1,0:T(8,128)}, f32[1,64,128]{2,1,0:T(8,128)}, f32[128,1024]{1,0:T(8,128)}) custom-call(bf16[2048,128]{1,0:T(8,128)(2,1)} %get-tuple-element.15.refs_0_, f32[1024,128]{1,0:T(8,128)} %get-tuple-element.16.refs_1_, f32[1024,128]{1,0:T(8,128)} %get-tuple-element.17.refs_2_, ...), custom_call_target="tpu_custom_call" | custom-call | tf_op jit(solution)/shard_map/grads/pallas_call | solution.py:637

commit v5 on v4

--- a/solution.py
+++ b/solution.py
@@ -513,7 +513,8 @@
         last.start(xs.at[:, part], xr.at[:, part], xss.at[r], xrs.at[r], p.other_pair())
         if r == 1:
             ar2.step3()
-    ar3.step3()
+        if r == 2:
+            ar3.step3()
     for r in range(NCHUNK):
         rows = pl.ds(r * CHUNK, CHUNK)
         own[:, rows] = dot(mt[1], st[:, rows])

time: 53.7 us -> 53.7 us (level)
  no operation moved by 1% of the time
where the time goes in v5:
time: 53.7 us; the launch traced here: 53.6 us
  Pallas kernels  52.1 us (97%)
  between operations  1.45 us (3%)
    pallas_call x1, Pallas kernels, shards(): pl.pallas_call(main_kernel, name='layer', out_shape=shapes, in_specs=[hbm...  49.7 us
    pallas_call x1, Pallas kernels, shards(): pl.pallas_call(finish_kernel, name='grads', out_shape=shapes, in_specs=[h...  2.45 us

profile of v5, /device:TPU:1, one launch (start us, length us, event | category | flops | bytes accessed | tf_op | source)
XLA Modules:
  0.0 53.6 jit_solution(6062200844286946847)
XLA Ops:
  1.3 49.7 %layer.1 = (bf16[2048,128]{1,0:T(8,128)(2,1)}, f32[1024,128]{1,0:T(8,128)}, f32[1024,128]{1,0:T(8,128)}, f32[1,64,128]{2,1,0:T(8,128)}, f32[128,1024]{1,0:T(8,128)}) custom-call(bf16[2048,1024]{1,0:T(8,128)(2,1)} %cells_h.1, bf16[2048,1024]{1,0:T(8,128)(2,1)} %cot_h.1, s32[1]{0:T(128)S(6)} %copy.15.counts, bf16[1024,128]{1,0:T(8,128)(2,1)} %fx_h.1, ...), custom_call_target="tpu_custom_call" | custom-call | tf_op jit(solution)/shard_map/layer/pallas_call | solution.py:583
  51.0 2.5 %grads.1 = (bf16[2048,128]{1,0:T(8,128)(2,1)}, f32[1024,128]{1,0:T(8,128)}, f32[1024,128]{1,0:T(8,128)}, f32[1,64,128]{2,1,0:T(8,128)}, f32[128,1024]{1,0:T(8,128)}) custom-call(bf16[2048,128]{1,0:T(8,128)(2,1)} %get-tuple-element.15.refs_0_, f32[1024,128]{1,0:T(8,128)} %get-tuple-element.16.refs_1_, f32[1024,128]{1,0:T(8,128)} %get-tuple-element.17.refs_2_, ...), custom_call_target="tpu_custom_call" | custom-call | tf_op jit(solution)/shard_map/grads/pallas_call | solution.py:638
